TPU v7x, 32 devices: a whole 2x2x4 slice. The times are simulated.
32 devices in a mesh: groups: 2 (over y), dom: 4 (over z), cls: 2 (over x), coef: 2 (over core).
Axes of the slice: x: 2, y: 2, z: 4, core: 2. Of those that a mesh axis runs over, the one named last changes fastest.
Arguments:
- particles: bfloat16 [3584, 2, 5120], P(('groups', 'dom', 'cls'), None, 'coef'), parts along dimension 0, may hold values from -6 to 6
- classes: int32 [3584, 1], P(('groups', 'dom', 'cls')), parts along dimension 0, may hold values from 0 to 255; in each aligned block of 224 rows (0 to 223, 224 to 447, ...) at most 2 rows name the same one
- angles: int32 [3584], P(('groups', 'dom', 'cls')), parts along dimension 0, may hold values from 0 to 359
- counts: int32 [3584], P(('groups', 'dom', 'cls')), parts along dimension 0, may hold values from 1 to 8
Outputs:
- averages: bfloat16 [512, 2, 5120], P(('groups', 'dom', 'cls'), None, 'coef'), parts along dimension 0
- gains: float32 [3584], P(('groups', 'dom', 'cls')), parts along dimension 0
There are 2 independent parts, one for each index of `groups`. A program takes and returns all parts, laid end to end along the dimension named above; each array names one. Nothing has to cross between parts.
Inputs may be any that keep to these rules, and one draw needn't show every extreme that they name: `classes`: in each device's aligned block of 224 particles no class holds more than 2 particles, and some class holds exactly 2; every class holds at least one particle of the part.
All inputs are finite; a program needn't handle non-finite values.
Results may differ from a plain program's by a relative error of at most 0.0014.
Values may be sent and summed in bfloat16 or wider, within the bound.
No kernel may reach another device: no remote copies, remote signals or barrier semaphores. Data moves between devices by JAX's collectives and lax.ppermute only.
A program may use at most 64 MiB of HBM per device.

v0:
```python
import math

import jax
import jax.numpy as jnp
from jax import lax
from jax.sharding import PartitionSpec as P

NK = 80
NQ = 64
CLASSES = 256
CAP = 2


def rotation(angle, first, width):
    frequency = first + jnp.arange(width, dtype=jnp.int32) // NQ
    turns = angle[..., None] * frequency % 360
    theta = turns.astype(jnp.float32) * (2.0 * math.pi / 360.0)
    return (jnp.cos(theta), jnp.sin(theta))


def shards(particles, classes, angles, counts):
    n_dom = lax.axis_size("dom")
    n_cls = lax.axis_size("cls")
    devices = n_dom * n_cls
    rows = particles.shape[0]
    width = particles.shape[2]
    local_freq = width // NQ
    first = lax.axis_index("coef") * local_freq
    labels = classes[:, 0]
    order = jnp.arange(rows, dtype=jnp.int32)
    earlier = (labels[:, None] == labels[None, :]) & (order[None, :] < order[:, None])
    rank = jnp.sum(earlier.astype(jnp.int32), axis=1)
    slot = labels * CAP + rank
    slots = CLASSES * CAP
    per_dest = slots // devices
    owned = per_dest // CAP
    place = jnp.arange(slots, dtype=jnp.int32)[:, None] == slot[None, :]
    packed = jnp.dot(
        place.astype(jnp.bfloat16),
        particles.reshape(rows, 2 * width),
        preferred_element_type=jnp.float32,
    ).astype(jnp.bfloat16)
    details = jnp.stack([angles, counts], axis=1)
    slot_details = jnp.sum(jnp.where(place[:, :, None], details[None, :, :], 0), axis=1)
    arrived, arrived_details = (
        lax.all_to_all(
            packed.reshape(devices, per_dest, 2 * width),
            ("dom", "cls"),
            split_axis=0,
            concat_axis=0,
            tiled=True,
        ),
        lax.all_to_all(
            slot_details.reshape(devices, per_dest, 2),
            ("dom", "cls"),
            split_axis=0,
            concat_axis=0,
            tiled=True,
        ),
    )
    arrived = arrived.reshape(devices, owned, CAP, 2, width)
    arrived_details = arrived_details.reshape(devices, owned, CAP, 2)
    cosine, sine = rotation(arrived_details[..., 0], first, width)
    weight = arrived_details[..., 1].astype(jnp.float32)
    real_part = arrived[:, :, :, 0].astype(jnp.float32)
    imag_part = arrived[:, :, :, 1].astype(jnp.float32)
    factor = weight[..., None]
    aligned_re = factor * (real_part * cosine - imag_part * sine)
    aligned_im = factor * (real_part * sine + imag_part * cosine)
    sums = jnp.stack([jnp.sum(aligned_re, axis=(0, 2)), jnp.sum(aligned_im, axis=(0, 2))], axis=1)
    totals = jnp.sum(weight, axis=(0, 2))
    averages = (sums / totals[:, None, None]).astype(jnp.bfloat16)
    piece = lax.all_gather(averages, ("dom", "cls"), axis=0, tiled=True)
    count = piece.shape[0]
    chooser = (labels[:, None] == jnp.arange(count, dtype=jnp.int32)[None, :]).astype(jnp.bfloat16)
    chosen = jnp.dot(chooser, piece.reshape(count, 2 * width), preferred_element_type=jnp.float32)
    chosen = chosen.reshape(rows, 2, width)
    own_cos, own_sin = rotation(angles, first, width)
    own_re = particles[:, 0].astype(jnp.float32)
    own_im = particles[:, 1].astype(jnp.float32)
    mean_re = chosen[:, 0]
    mean_im = chosen[:, 1]
    back_re = mean_re * own_cos + mean_im * own_sin
    back_im = mean_im * own_cos - mean_re * own_sin
    term = 2.0 * (own_re * back_re + own_im * back_im) - (mean_re * mean_re + mean_im * mean_im)
    whole = lax.psum(jnp.sum(term, axis=1), "coef")
    gain = whole / math.sqrt(2.0 * NK * NQ)
    return (averages, gain)


def solution(mesh):
    in_specs = (
        P(("groups", "dom", "cls"), None, "coef"),
        P(("groups", "dom", "cls"), None),
        P(("groups", "dom", "cls")),
        P(("groups", "dom", "cls")),
    )
    out_specs = (P(("groups", "dom", "cls"), None, "coef"), P(("groups", "dom", "cls")))
    return jax.shard_map(shards, mesh=mesh, in_specs=in_specs, out_specs=out_specs, check_vma=False)
```

profile of v0, /device:TPU:0, one launch (start us, length us, event | category | flops | bytes accessed | tf_op | source)
XLA Modules:
  0.0 346.9 jit_solution(13669090917482610930)
XLA Ops:
  7.2 0.9 convert_reduce_fusion
  8.1 0.7 multiply_add_fusion
  8.8 0.1 iota_compare_fusion
  8.9 0.7 pad_add_fusion
  9.6 0.2 select_reduce_fusion
  9.8 0.1 reshape.92
  9.9 0.7 reshape.103
  10.6 7.3 %all-to-all-start = ((s32[8,1,128]{2,1,0:T(1,128)}), s32[8,1,128]{2,1,0:T(1,128)S(1)}, u32[]{:S(2)}, u32[]{:S(2)}) async-start(s32[8,1,128]{2,1,0:T(1,128)} %reshape.103), calls=%async_computation | async-start | bytes 8192 | tf_op jit(solution)/shard_map/all_to_all | solution.py:53
  17.8 2.0 copy.49
  19.8 4.0 %convolution_convert_fusion = bf16[512,5120]{1,0:T(8,128)(2,1)} fusion(bf16[224,5120]{1,0:T(8,128)(2,1)S(1)} %bitcast.68, s32[224]{0:T(256)S(1)} %multiply_add_fusion), kind=kOutput, calls=%fused_computation.1 | convolution fusion | flops 1177141248 | bytes 7537536 | tf_op jit(solution)/shard_map/dot_general | solution.py:38
  23.8 0.4 all-to-all-done
  24.2 5.6 %all-to-all-start.1 = ((bf16[8,64,5120]{2,1,0:T(8,128)(2,1)}), bf16[8,64,5120]{2,1,0:T(8,128)(2,1)}, u32[]{:S(2)}, u32[]{:S(2)}) async-start(bf16[8,64,5120]{2,1,0:T(8,128)(2,1)} %bitcast.66), calls=%async_computation.1 | async-start | bytes 10485760 | tf_op jit(solution)/shard_map/all_to_all | solution.py:46
  29.8 0.2 all-gather.2.cloned.1.call-start
  30.1 0.5 broadcast.83
  30.6 0.7 reduce.1
  31.2 0.1 reshape.104
  31.3 0.1 copy.37
  31.4 0.3 copy.40
  31.7 0.3 copy.38
  32.0 0.3 fusion.26
  32.3 112.7 %all-to-all-done.1 = bf16[8,64,5120]{2,1,0:T(8,128)(2,1)} async-done(((bf16[8,64,5120]{2,1,0:T(8,128)(2,1)}), bf16[8,64,5120]{2,1,0:T(8,128)(2,1)}, u32[]{:S(2)}, u32[]{:S(2)}) %all-to-all-start.1) | async-done | bytes 5242912 | tf_op jit(solution)/shard_map/all_to_all | solution.py:46
  145.0 12.4 %reshape.96 = bf16[8,32,2,2,2560]{4,3,2,1,0:T(2,128)(2,1)} reshape(bf16[8,64,5120]{2,1,0:T(8,128)(2,1)} %all-to-all-done.1) | data formatting | bytes 10485760 | tf_op jit(solution)/shard_map/reshape | solution.py:61
  157.4 10.8 %fusion.32 = (bf16[8,32,2,1,2560]{4,3,2,1,0:T(2,128)(2,1)S(1)}, f32[8,32,2,1,2560]{4,3,2,1,0:T(1,128)S(1)}) fusion(bf16[8,32,2,2,2560]{4,3,2,1,0:T(2,128)(2,1)} %reshape.96), kind=kLoop, calls=%fused_computation.62 | loop fusion | flops 1310720 | bytes 13107200 | tf_op jit(solution)/shard_map/slice | solution.py:65
  168.2 0.0 copy-start
  168.2 97.8 %fusion.7 = (f32[32,2560]{1,0:T(8,128)S(1)}, f32[32,2560]{1,0:T(8,128)S(1)}) fusion(f32[8,32,2,1,2560]{4,3,2,1,0:T(1,128)S(1)} %get-tuple-element.13, s32[2560]{0:T(1024)S(1)} %fusion.28, s32[8,32,2]{2,1,0:T(8,128)S(1)} %copy.40, f32[8,32,2]{2,1,0:T(8,128)S(1)} %copy.38, bf16[8,32,2,1,2560]{4,3,2,1,0:T(2,128)(2,1)S(1)} %get-tuple-element.12), kind=kLoop, calls=%fused_computation.14 | loop fusion | flops 26050560 | bytes 8534016 | tf_op jit(solution)/shard_map/reduce_sum | solution.py:70
  266.0 0.8 fusion.21
  266.8 0.0 all-gather.2.cloned.1.call-update
  266.9 0.0 copy-done
  266.9 0.0 copy-start.3
  266.9 4.5 %fusion.33 = (bf16[224,1,2560]{2,1,0:T(2,128)(2,1)}, bf16[224,1,2560]{2,1,0:T(2,128)(2,1)}) fusion(bf16[224,2,2560]{2,1,0:T(2,128)(2,1)S(1)} %copy-done), kind=kLoop, calls=%fused_computation.63 | loop fusion | bytes 4587520 | tf_op jit(solution)/shard_map/slice | solution.py:79
  271.4 0.0 copy-done.3
  271.4 1.1 copy.44
  272.4 0.0 copy-start.4
  272.4 48.3 %all-gather.2.cloned.1.call-done = bf16[256,2,2560]{2,0,1:T(8,128)(2,1)} async-done(((bf16[32,2,2560]{2,0,1:T(8,128)(2,1)}), bf16[256,2,2560]{2,0,1:T(8,128)(2,1)}) %all-gather.2.cloned.1.call-update) | async-done | bytes 2621456 | tf_op jit(solution)/shard_map/all_gather | solution.py:73
  320.8 3.0 copy.42
  323.7 0.0 copy-done.4
  323.7 0.0 copy-start.1
  323.8 0.0 copy-start.2
  323.8 0.0 copy-start.5
  323.8 1.0 fusion.8
  324.8 0.6 copy-done.1
  325.4 0.7 copy-done.2
  326.1 0.0 copy-done.5
  326.1 11.0 %fusion.17 = f32[224]{0:T(256)S(1)} fusion(f32[224,2,2560]{2,0,1:T(8,128)S(1)} %fusion.8, bf16[224,1,2560]{2,1,0:T(2,128)(2,1)S(1)} %copy-done.2, bf16[224,1,2560]{2,1,0:T(2,128)(2,1)S(1)} %copy-done.1, s32[2560]{0:T(1024)S(1)} %fusion.28, s32[224]{0:T(256)S(1)} %copy-done.5), kind=kLoop, calls=%fused_computation.29 | loop fusion | flops 14909216 | bytes 6893312 | tf_op jit(solution)/shard_map/reduce_sum | solution.py:86
  337.0 2.5 psum.7
  339.5 0.6 broadcast_multiply_fusion
  (3 shorter events, 0.0 us)
Async XLA Ops:
  10.6 13.6 %all-to-all-start = ((s32[8,1,128]{2,1,0:T(1,128)}), s32[8,1,128]{2,1,0:T(1,128)S(1)}, u32[]{:S(2)}, u32[]{:S(2)}) async-start(s32[8,1,128]{2,1,0:T(1,128)} %reshape.103), calls=%async_computation | async-start | bytes 8192 | tf_op jit(solution)/shard_map/all_to_all | solution.py:53
  24.2 120.8 %all-to-all-start.1 = ((bf16[8,64,5120]{2,1,0:T(8,128)(2,1)}), bf16[8,64,5120]{2,1,0:T(8,128)(2,1)}, u32[]{:S(2)}, u32[]{:S(2)}) async-start(bf16[8,64,5120]{2,1,0:T(8,128)(2,1)} %bitcast.66), calls=%async_computation.1 | async-start | bytes 10485760 | tf_op jit(solution)/shard_map/all_to_all | solution.py:46
  29.8 290.9 %all-gather.2.cloned.1.call-start = ((), (), s32[]{:S(2)}) async-start(), calls=%async_computation.2 | async-start | bytes 2949120 | tf_op jit(solution)/shard_map/all_gather | solution.py:73
  168.2 98.7 %copy-start = (bf16[224,2,2560]{2,1,0:T(2,128)(2,1)S(1)}, bf16[224,2,2560]{2,1,0:T(2,128)(2,1)}, u32[]{:S(2)}) copy-start(bf16[224,2,2560]{2,1,0:T(2,128)(2,1)} %param.4) | copy-start | bytes 6881284
  266.9 4.5 %copy-start.3 = (bf16[32,2,2560]{2,0,1:T(8,128)(2,1)S(1)}, bf16[32,2,2560]{2,0,1:T(8,128)(2,1)}, u32[]{:S(2)}) copy-start(bf16[32,2,2560]{2,0,1:T(8,128)(2,1)} %fusion.21) | copy-start | bytes 983044
  272.4 51.3 %copy-start.4 = (s32[224,1]{0,1:T(1,128)S(1)}, s32[224,1]{0,1:T(1,128)}, u32[]{:S(2)}) copy-start(s32[224,1]{0,1:T(1,128)} %param.5) | copy-start | bytes 2692
  323.7 1.6 copy-start.1
  323.8 2.3 copy-start.2
  323.8 2.3 copy-start.5
Sparse Core Ops, SparseCore 0:
  267.0 53.7 all-gather.1
where the time goes:
time: 348 us; the launch traced here: 347 us
  waiting for transfers between devices  161 us (46%)
  other arithmetic  125 us (36%)
  local copies, waits for them, and re-layouts  26.3 us (8%)
  between operations  14.2 us (4%)
  starting transfers between devices  13.1 us (4%)
  matrix products  5 us (1%)
    all_to_all x1, waiting for transfers between devices, shards(): lax.all_to_all(packed.reshape(devices, per_dest, 2 * width), ('dom', 'cls...  113 us
    reduce_sum x1, other arithmetic, shards(): jnp.sum(aligned_re, axis=(0, 2))  97.8 us
    all_gather x1, waiting for transfers between devices, shards(): piece = lax.all_gather(averages, ('dom', 'cls'), axis=0, tiled=True)  48.3 us
    reshape x1, local copies, waits for them, and re-layouts, shards(): arrived = arrived.reshape(devices, owned, CAP, 2, width)  12.4 us
    reduce_sum x1, other arithmetic, shards(): whole = lax.psum(jnp.sum(term, axis=1), 'coef')  11 us
    slice x1, other arithmetic, shards(): real_part = arrived[:, :, :, 0].astype(jnp.float32)  10.8 us
    all_to_all x1, starting transfers between devices, shards(): lax.all_to_all(slot_details.reshape(devices, per_dest, 2), ('dom', 'cls')...  7.25 us
  transfers between devices with their start and end apart: 3, of which 3 were waited for; matrix products, arithmetic and copies ran while one was open for 4% of the time, Pallas kernels for 0%

commit v1 on v0

v1 whole, which is shorter than its diff:
```python
import functools
import math

import jax
import jax.numpy as jnp
from jax import lax
from jax.experimental import pallas as pl
from jax.experimental.pallas import tpu as pltpu
from jax.sharding import PartitionSpec as P

NK = 80
NQ = 64
CLASSES = 256
CAP = 2
LANES = 128
BLOCK = 256
SHARES = (0.5, 0.5)
PARAMS = pltpu.CompilerParams(vmem_limit_bytes=48 << 20)
NT = (((1,), (1,)), ((), ()))
f32 = jnp.float32
bf16 = jnp.bfloat16
i32 = jnp.int32


def matmul(a, b, dims=(((1,), (0,)), ((), ()))):
    return lax.dot_general(a, b, dims, preferred_element_type=f32)


def split(value):
    high = value.astype(bf16)
    return high, (value - high.astype(f32)).astype(bf16)


def split3(value):
    high = value.astype(bf16)
    rest = value - high.astype(f32)
    mid = rest.astype(bf16)
    return high, mid, (rest - mid.astype(f32)).astype(bf16)


def place_of(slot, count):
    rows = lax.broadcasted_iota(i32, (count, slot.shape[1]), 0)
    return jnp.where(rows == slot, 1.0, 0.0).astype(bf16)


def pack_first(parts, cap, meta_ref, x_ref, *out_refs):
    slot_ref = out_refs[parts]
    people = meta_ref.shape[1]
    width = x_ref.shape[1]
    meta = meta_ref[...]
    dest = meta[0:1]
    chosen = jnp.where(lax.broadcasted_iota(i32, (16, people), 0) == dest, 1.0, 0.0)
    before = jnp.where(
        lax.broadcasted_iota(i32, (people, people), 0) < lax.broadcasted_iota(i32, (people, people), 1), 1.0, 0.0
    ).astype(bf16)
    ahead = matmul(chosen.astype(bf16), before)
    rank = jnp.sum(chosen * ahead, axis=0, keepdims=True).astype(i32)
    over = jnp.max(jnp.where(rank >= cap, 1.0, 0.0))
    slot = jnp.where(rank < cap, dest * cap + rank, -1)
    slot_ref[...] = jnp.broadcast_to(jnp.where(rank < cap, dest * LANES + rank, -1), slot_ref.shape)
    half = lax.shift_right_logical(meta[2:3], 1)
    rows = lax.broadcasted_iota(i32, (LANES, people), 0)
    details = jnp.where(rows == 0, meta[1:2], 0)
    details = jnp.where(rows == 1, half, details)
    details = jnp.where(rows == 2, meta[2:3] - 2 * half, details)
    details = jnp.where(rows == 3, meta[3:4], details)
    details = details.astype(f32).astype(bf16)
    lane = lax.broadcasted_iota(i32, (cap, LANES), 1)
    for part in range(parts):
        place = place_of(slot - part * cap, cap)
        out_refs[part][:, :width] = matmul(place, x_ref[...]).astype(bf16)
        block = jnp.where(lane == 4, over, matmul(place, details, NT))
        out_refs[part][:, width:] = block.astype(bf16)


def pack_next(parts, cap, slot_ref, x_ref, *out_refs):
    slot = slot_ref[0:1]
    dest = lax.shift_right_arithmetic(slot, 7)
    slot = jnp.where(slot >= 0, dest * cap + (slot - dest * LANES), -1)
    for part in range(parts):
        out_refs[part][...] = matmul(place_of(slot - part * cap, cap), x_ref[...]).astype(bf16)


def align(parts, cap, subs, nfreq, first, freqs, start, *refs):
    width = freqs * NQ
    taken, refs = refs[:parts], refs[parts:]
    if first:
        core_ref, code_ref, sums_ref, high_ref, mid_ref, cos_ref, sin_ref, hot_ref, info_ref = refs
        core = core_ref[0, 0]
        details = jnp.concatenate([ref[:, 2 * width :] for ref in taken], axis=0)
        columns = details.astype(f32)
        angle = 2.0 * columns[:, 1:2] + columns[:, 2:3]
        rows = parts * cap
        lane = lax.broadcasted_iota(i32, (rows, cos_ref.shape[1]), 1)
        third = jnp.where(lane >= nfreq, 1, 0) + jnp.where(lane >= 2 * nfreq, 1, 0)
        frequency = (lane - third * nfreq + core * nfreq).astype(f32)
        turns = angle * frequency
        turns = turns - 360.0 * jnp.floor((turns + 0.5) * (1.0 / 360.0))
        theta = turns * (2.0 * math.pi / 360.0)
        for table, ref in ((jnp.cos(theta), cos_ref), (jnp.sin(theta), sin_ref)):
            high, mid, low = [piece.astype(f32) for piece in split3(table)]
            ref[...] = jnp.where(third == 0, high, jnp.where(third == 1, mid, low)).astype(bf16)
        pick = jnp.where(
            lax.broadcasted_iota(i32, (16, LANES), 0) == lax.broadcasted_iota(i32, (16, LANES), 1), 1.0, 0.0
        ).astype(bf16)
        flat = matmul(pick, details, NT)
        hot = jnp.where(lax.broadcasted_iota(i32, (subs, rows), 0) == flat[0:1].astype(i32), 1.0, 0.0)
        hot_ref[0] = hot.astype(bf16)
        weighted = hot * flat[3:4]
        hot_ref[1] = weighted.astype(bf16)
        totals = jnp.sum(weighted, axis=1, keepdims=True)
        over = jnp.max(flat[4:5])
        slot = lax.broadcasted_iota(i32, info_ref.shape, 1)
        info_ref[...] = jnp.where(slot == 1, totals, jnp.where(slot == 2, over, 0.0))
    else:
        cos_ref, sin_ref, hot_ref, code_ref, sums_ref, high_ref, mid_ref = refs
        info_ref = None
    lanes = cos_ref.shape[1]
    weights = hot_ref[1]
    cosines, sines = cos_ref[...], sin_ref[...]
    row = lax.broadcasted_iota(i32, (lanes, BLOCK), 0)
    row = row - jnp.where(row >= nfreq, nfreq, 0) - jnp.where(row >= 2 * nfreq, nfreq, 0)
    lane_freq = lax.shift_right_logical(lax.broadcasted_iota(i32, (lanes, BLOCK), 1), 6)
    inside = lax.broadcasted_iota(i32, (lanes, BLOCK), 0) < 3 * nfreq
    for block in range(width // BLOCK):
        at = pl.ds(block * BLOCK, BLOCK)
        at_im = pl.ds(width + block * BLOCK, BLOCK)
        spread = jnp.where(inside & (row == lane_freq + (start + block * (BLOCK // NQ))), 1.0, 0.0).astype(bf16)
        cosine, sine = matmul(cosines, spread), matmul(sines, spread)
        real = jnp.concatenate([ref[:, at] for ref in taken], axis=0).astype(f32)
        imag = jnp.concatenate([ref[:, at_im] for ref in taken], axis=0).astype(f32)
        for here, value in ((at, real * cosine - imag * sine), (at_im, real * sine + imag * cosine)):
            high, mid = split(value)
            high_ref[:, here] = high
            mid_ref[:, here] = mid
            sums_ref[:, here] = matmul(weights, high) + matmul(weights, mid)
    largest = jnp.maximum(jnp.max(jnp.abs(sums_ref[...]), axis=1, keepdims=True), 1e-30)
    level = jnp.ceil(jnp.log(largest) * (4.0 / math.log(2.0)) + 0.02)
    coded = jnp.floor(sums_ref[...] * jnp.exp2(15.0 - 0.25 * level) + 0.5)
    code_ref[:, : 2 * width] = coded.astype(i32).astype(jnp.int16)
    slot = lax.broadcasted_iota(i32, (subs, LANES), 1)
    extra = jnp.where(slot == 0, level, 0.0 if info_ref is None else info_ref[...])
    code_ref[:, 2 * width :] = extra.astype(i32).astype(jnp.int16)


def score(parts, cap, others, first, last, *refs):
    codes, refs = refs[:others], refs[others:]
    sums_ref, high_ref, mid_ref, hot_ref, info_ref, refs = *refs[:5], refs[5:]
    if first:
        mean_ref, total_ref, gain_ref = refs
        info = info_ref[...]
        for code_ref in codes:
            more = code_ref[:, sums_ref.shape[1] :].astype(i32).astype(f32)
            slot = lax.broadcasted_iota(i32, more.shape, 1)
            info = info + jnp.where(slot == 0, 0.0, more)
        total_ref[...] = info
        so_far = None
    else:
        so_far_ref, mean_ref, gain_ref = refs
        info = info_ref[...]
        so_far = so_far_ref[0:1]
    wide = sums_ref.shape[1]
    sums = sums_ref[...]
    for code_ref in codes:
        level = code_ref[:, wide:].astype(i32).astype(f32)[:, 0:1]
        sums = sums + code_ref[:, :wide].astype(i32).astype(f32) * jnp.exp2(0.25 * level - 15.0)
    mean = (sums / info[:, 1:2]).astype(bf16)
    mean_ref[...] = mean
    wide_mean = mean.astype(f32)
    norm = jnp.sum(wide_mean * wide_mean, axis=1, keepdims=True)
    product = matmul(mean, high_ref[...], NT) + matmul(mean, mid_ref[...], NT)
    gain = jnp.sum(hot_ref[0].astype(f32) * (2.0 * product - norm), axis=0, keepdims=True)
    if so_far is not None:
        gain = gain + so_far
    if last:
        gain_ref[...] = jnp.zeros(gain_ref.shape, f32)
        for part in range(parts):
            gain_ref[part : part + 1, :cap] = gain[:, part * cap : (part + 1) * cap]
    else:
        gain_ref[...] = jnp.broadcast_to(gain, gain_ref.shape)


def unpack(parts, slot_ref, *refs):
    returned, out_ref = refs[:parts], refs[parts]
    slot = slot_ref[0:1]
    total = jnp.zeros((8, slot.shape[1]), f32)
    for part in range(parts):
        place = place_of(slot - part * LANES, LANES)
        mine = jnp.broadcast_to(returned[part][part : part + 1], (8, LANES))
        for piece in split3(mine):
            total = total + matmul(piece, place)
    out_ref[...] = total[0:1] * (1.0 / math.sqrt(2.0 * NK * NQ))


def call(kernel, outs, *args):
    shapes = [jax.ShapeDtypeStruct(shape, dtype) for shape, dtype in outs]
    return pl.pallas_call(kernel, out_shape=shapes, compiler_params=PARAMS)(*args)


def exchange(cap, particles, meta, square, n_dom, n_cls, pair):
    people, _, width = particles.shape
    axes = ("dom", "cls")
    parts = pair * n_cls
    groups = n_dom // pair
    owned = CLASSES // (n_dom * n_cls)
    subs = groups * owned
    rows = parts * cap
    nfreq = width // NQ
    step = BLOCK // NQ
    sizes = [max(step, int(nfreq * share) // step * step) for share in SHARES[:-1]]
    sizes.append(nfreq - sum(sizes))
    devices = [(z, x) for z in range(n_dom) for x in range(n_cls)]

    def forward(part):
        dz, dx = divmod(part, n_cls)
        return [(z * n_cls + x, (z ^ dz) * n_cls + (x + dx) % n_cls) for z, x in devices]

    def across(turn):
        return [(z * n_cls + x, ((z // pair + turn) % groups * pair + z % pair) * n_cls + x) for z, x in devices]

    def deliver(packed):
        sent = [lax.ppermute(packed[part], axes, forward(part)) for part in range(1, parts)]
        return [packed[0], *sent]

    lanes = -(-3 * nfreq // LANES) * LANES
    starts = [sum(sizes[:i]) for i in range(len(sizes))]
    core = lax.axis_index("coef").reshape(1, 1).astype(i32)
    arrived = []
    slot = None
    for number, (start, freqs) in enumerate(zip(starts, sizes)):
        x = particles[:, :, start * NQ : (start + freqs) * NQ].reshape(people, 2 * freqs * NQ)
        if number == 0:
            *packed, slot = call(
                functools.partial(pack_first, parts, cap),
                [((cap, 2 * freqs * NQ + LANES), bf16)] * parts + [((8, people), i32)],
                meta,
                x,
            )
        else:
            packed = call(
                functools.partial(pack_next, parts, cap), [((cap, 2 * freqs * NQ), bf16)] * parts, slot, x
            )
        arrived.append(deliver(packed))
    aligned = []
    for number, (start, freqs) in enumerate(zip(starts, sizes)):
        wide = 2 * freqs * NQ
        kernel = functools.partial(align, parts, cap, subs, nfreq, number == 0, freqs, start)
        outs = [
            ((subs, wide + LANES), jnp.int16),
            ((subs, wide), f32),
            ((rows, wide), bf16),
            ((rows, wide), bf16),
        ]
        if number == 0:
            more = [((rows, lanes), bf16)] * 2 + [((2, subs, rows), bf16), ((subs, LANES), f32)]
            specs = [pl.BlockSpec(memory_space=pltpu.VMEM)] * parts + [pl.BlockSpec(memory_space=pltpu.SMEM)]
            code, sums, high, mid, cosines, sines, hot, info = pl.pallas_call(
                kernel,
                in_specs=specs,
                out_shape=[jax.ShapeDtypeStruct(*out) for out in outs + more],
                compiler_params=PARAMS,
            )(*arrived[0], core)
        else:
            code, sums, high, mid = call(kernel, outs, *arrived[number], cosines, sines, hot)
        codes = [lax.ppermute(code, axes, across(turn)) for turn in range(1, groups)]
        aligned.append((codes, sums, high, mid))
    means = []
    gain = None
    for number, (codes, sums, high, mid) in enumerate(aligned):
        first, last = number == 0, number == len(sizes) - 1
        kernel = functools.partial(score, parts, cap, groups - 1, first, last)
        outs = [(sums.shape, bf16)]
        outs += [((subs, LANES), f32)] if first else []
        outs += [((-(-parts // 8) * 8, LANES), f32) if last else ((8, rows), f32)]
        args = [*codes, sums, high, mid, hot, info]
        if first:
            mean, *rest = call(kernel, outs, *args)
            info = rest[0]
            gain = rest[1]
        else:
            mean, gain = call(kernel, outs, *args, gain)
        means.append(mean)
    gain = lax.psum(gain, "coef")
    returned = [gain]
    for part in range(1, parts):
        returned.append(lax.ppermute(gain, axes, [(b, a) for a, b in forward(part)]))
    (gains,) = call(functools.partial(unpack, parts), [((1, people), f32)], slot, *returned)
    mine = [
        lax.dynamic_slice_in_dim(mean, square * owned, owned).reshape(owned, 2, -1) for mean in means
    ]
    averages = jnp.concatenate(mine, axis=2)
    return averages, gains.reshape(people), info[0, 2] > 0.0


def shards(particles, classes, angles, counts):
    n_dom = lax.axis_size("dom")
    n_cls = lax.axis_size("cls")
    pair = 2 if n_dom % 2 == 0 else 1
    z, x = lax.axis_index("dom"), lax.axis_index("cls")
    people = particles.shape[0]
    owned = CLASSES // (n_dom * n_cls)
    subs = n_dom // pair * owned
    parts = pair * n_cls
    label = classes.reshape(1, people)
    owner = label // owned
    z_of, x_of = owner // n_cls, owner % n_cls
    dest = (z_of % pair + pair - z % pair) % pair * n_cls + (x_of + n_cls - x) % n_cls
    index = z_of // pair * owned + label % owned
    meta = jnp.concatenate([dest, index, angles[None], counts[None], jnp.zeros((4, people), i32)], axis=0)
    mean_rows = people / parts
    most = min(CAP * subs, people + 15) // 16 * 16
    cap = min(most, -(-int(mean_rows + 3.2 * math.sqrt(mean_rows)) // 16) * 16)
    run = functools.partial(exchange, n_dom=n_dom, n_cls=n_cls, pair=pair)
    averages, gains, over = run(cap, particles, meta, z // pair)
    if cap == most:
        return averages, gains
    return lax.cond(
        over,
        lambda: run(most, particles, meta, z // pair)[:2],
        lambda: (averages, gains),
    )


def solution(mesh):
    in_specs = (
        P(("groups", "dom", "cls"), None, "coef"),
        P(("groups", "dom", "cls"), None),
        P(("groups", "dom", "cls")),
        P(("groups", "dom", "cls")),
    )
    out_specs = (P(("groups", "dom", "cls"), None, "coef"), P(("groups", "dom", "cls")))
    return jax.shard_map(shards, mesh=mesh, in_specs=in_specs, out_specs=out_specs, check_vma=False)
```

time: 348 us -> 94.5 us (0.27)
  waiting for transfers between devices: 161 us -> 32.6 us
  other arithmetic: 125 us -> 1.01 us
  Pallas kernels: 0 us -> 15.6 us
  between operations: 14.2 us -> 1.48 us
  starting transfers between devices: 13.1 us -> 20.3 us
  local copies, waits for them, and re-layouts: 26.3 us -> 20.5 us
  matrix products: 5 us -> 0 us
    all_to_all x2 -> x0, waiting for transfers between devices: 113 us -> none  [the longest x1 113 us: shards(): lax.all_to_all(packed.reshape(devices, per_dest, 2 * width), ('dom', 'cls...]
    reduce_sum x5 -> x0, other arithmetic: 110 us -> none  [the longest x1 97.8 us: shards(): jnp.sum(aligned_re, axis=(0, 2))]
    all_gather x1 -> x0, waiting for transfers between devices: 48.3 us -> none  [shards(): piece = lax.all_gather(averages, ('dom', 'cls'), axis=0, tiled=True)]
    ppermute x0 -> x11, waiting for transfers between devices: none -> 32.6 us  [the longest x6 23.2 us: deliver(): lax.ppermute(packed[part], axes, forward(part))]
    ppermute x0 -> x11, starting transfers between devices: none -> 20.3 us  [the longest x6 11.8 us: deliver(): lax.ppermute(packed[part], axes, forward(part))]
    pallas_call x0 -> x7, Pallas kernels: none -> 15.6 us  [the longest x6 11.2 us: call(): pl.pallas_call(kernel, out_shape=shapes, compiler_params=PARAMS)(*args)]
    all_to_all x2 -> x0, starting transfers between devices: 12.8 us -> none  [the longest x1 7.25 us: shards(): lax.all_to_all(slot_details.reshape(devices, per_dest, 2), ('dom', 'cls')...]
    reshape x3 -> x2, local copies, waits for them, and re-layouts: 12.5 us -> 0.09 us  [exchange(): lax.dynamic_slice_in_dim(mean, square * owned, owned).reshape(owned, 2, -1)]
  transfers between devices with their start and end apart: 3 -> 11, of which waited for: 3 -> 5; matrix products, arithmetic and copies ran while one was open for 4% -> 3% of each run, Pallas kernels for 0% -> 12%
where the time goes in v1:
time: 94.5 us; the launch traced here: 94 us
  waiting for transfers between devices  32.6 us (34%)
  local copies, waits for them, and re-layouts  20.5 us (22%)
  starting transfers between devices  20.3 us (21%)
  Pallas kernels  15.6 us (17%)
  blocking collectives  2.44 us (3%)
  between operations  1.48 us (2%)
  other arithmetic  1.01 us (1%)
    ppermute x6, waiting for transfers between devices, deliver(): lax.ppermute(packed[part], axes, forward(part))  23.2 us
    unnamed x44, local copies, waits for them, and re-layouts  15 us
    ppermute x6, starting transfers between devices, deliver(): lax.ppermute(packed[part], axes, forward(part))  11.8 us
    pallas_call x6, Pallas kernels, call(): pl.pallas_call(kernel, out_shape=shapes, compiler_params=PARAMS)(*args)  11.2 us
    ppermute x2, waiting for transfers between devices, exchange(): lax.ppermute(code, axes, across(turn))  9.38 us
    ppermute x2, starting transfers between devices, exchange(): lax.ppermute(code, axes, across(turn))  5.05 us
    pallas_call x1, Pallas kernels, exchange(): pl.pallas_call(kernel, in_specs=specs, out_shape=[jax.ShapeDtypeStruct(*o...  4.35 us
    ppermute x3, starting transfers between devices, exchange(): lax.ppermute(gain, axes, [(b, a) for a, b in forward(part)])  3.49 us
  transfers between devices with their start and end apart: 11, of which 5 were waited for; matrix products, arithmetic and copies ran while one was open for 3% of the time, Pallas kernels for 12%

profile of v1, /device:TPU:0, one launch (start us, length us, event | category | flops | bytes accessed | tf_op | source)
XLA Modules:
  0.0 94.0 jit_solution(6214179452664932469)
XLA Ops:
  0.6 0.7 fusion.1
  1.4 2.9 %fusion.10 = (bf16[224,2,1280]{2,1,0:T(2,128)(2,1)S(1)}, bf16[224,2,1280]{2,1,0:T(2,128)(2,1)S(1)}) fusion(bf16[224,2,2560]{2,1,0:T(2,128)(2,1)} %param.6), kind=kLoop, calls=%fused_computation.38 | loop fusion | bytes 4587520 | tf_op jit(solution)/shard_map/slice | solution.py:231
  4.2 0.1 copy.8
  4.4 0.5 copy-done.25
  4.9 0.0 copy-done.26
  4.9 1.8 %shard_map.59 = (bf16[80,2688]{1,0:T(8,128)(2,1)S(1)}, bf16[80,2688]{1,0:T(8,128)(2,1)S(1)}, bf16[80,2688]{1,0:T(8,128)(2,1)}, bf16[80,2688]{1,0:T(8,128)(2,1)}, s32[8,224]{1,0:T(8,128)S(1)}) custom-call(s32[8,224]{1,0:T(8,128)S(1)} %concatenate.9.meta_ref, bf16[224,2560]{1,0:T(8,128)(2,1)S(1)} %bitcast.30), custom_call_target="tpu_custom_call" | custom-call | tf_op jit(solution)/shard_map/pallas_call | solution.py:197
  6.7 2.9 %collective-permute-start.11 = (bf16[80,2688]{1,0:T(8,128)(2,1)S(1)}, bf16[80,2688]{1,0:T(8,128)(2,1)S(1)}, u32[]{:S(2)}, u32[]{:S(2)}) collective-permute-start(bf16[80,2688]{1,0:T(8,128)(2,1)S(1)} %get-tuple-element.73), channel_id=1, source_target_pairs={{0,2},{2,0},{4,6},{6,4},{8,10},{10,8},{12,14},{14,12},{1,3},{3,1},... | collective-permute-start | bytes 1290248 | tf_op jit(solution)/shard_map/ppermute | solution.py:222
  9.7 1.6 %collective-permute-start.12 = (bf16[80,2688]{1,0:T(8,128)(2,1)}, bf16[80,2688]{1,0:T(8,128)(2,1)S(1)}, u32[]{:S(2)}, u32[]{:S(2)}) collective-permute-start(bf16[80,2688]{1,0:T(8,128)(2,1)} %get-tuple-element.74), channel_id=1, source_target_pairs={{0,4},{2,6},{4,0},{6,2},{8,12},{10,14},{12,8},{14,10},{1,5},{3,7},... | collective-permute-start | bytes 1290248 | tf_op jit(solution)/shard_map/ppermute | solution.py:222
  11.2 0.1 copy.9
  11.4 1.7 %shard_map.62 = (bf16[80,2560]{1,0:T(8,128)(2,1)S(1)}, bf16[80,2560]{1,0:T(8,128)(2,1)}, bf16[80,2560]{1,0:T(8,128)(2,1)}, bf16[80,2560]{1,0:T(8,128)(2,1)}) custom-call(s32[8,224]{1,0:T(8,128)S(1)} %get-tuple-element.83.slot_ref, bf16[224,2560]{1,0:T(8,128)(2,1)S(1)} %bitcast.32), custom_call_target="tpu_custom_call" | custom-call | tf_op jit(solution)/shard_map/pallas_call | solution.py:197
  13.1 0.8 copy-done.13
  13.8 1.9 %collective-permute-start.15 = (bf16[80,2560]{1,0:T(8,128)(2,1)}, bf16[80,2560]{1,0:T(8,128)(2,1)S(1)}, u32[]{:S(2)}, u32[]{:S(2)}) collective-permute-start(bf16[80,2560]{1,0:T(8,128)(2,1)} %get-tuple-element.85), channel_id=1, source_target_pairs={{0,2},{2,0},{4,6},{6,4},{8,10},{10,8},{12,14},{14,12},{1,3},{3,1},... | collective-permute-start | bytes 1228808 | tf_op jit(solution)/shard_map/ppermute | solution.py:222
  15.7 1.6 %collective-permute-start.16 = (bf16[80,2560]{1,0:T(8,128)(2,1)}, bf16[80,2560]{1,0:T(8,128)(2,1)S(1)}, u32[]{:S(2)}, u32[]{:S(2)}) collective-permute-start(bf16[80,2560]{1,0:T(8,128)(2,1)} %get-tuple-element.86), channel_id=1, source_target_pairs={{0,4},{2,6},{4,0},{6,2},{8,12},{10,14},{12,8},{14,10},{1,5},{3,7},... | collective-permute-start | bytes 1228808 | tf_op jit(solution)/shard_map/ppermute | solution.py:222
  17.3 3.6 %collective-permute-done.11.refs_1_ = bf16[80,2688]{1,0:T(8,128)(2,1)S(1)} collective-permute-done((bf16[80,2688]{1,0:T(8,128)(2,1)S(1)}, bf16[80,2688]{1,0:T(8,128)(2,1)S(1)}, u32[]{:S(2)}, u32[]{:S(2)}) %collective-permute-start.11) | collective-permute-done | bytes 430112 | tf_op jit(solution)/shard_map/ppermute | solution.py:222
  20.9 3.8 %collective-permute-start.17 = (bf16[80,2560]{1,0:T(8,128)(2,1)}, bf16[80,2560]{1,0:T(8,128)(2,1)S(1)}, u32[]{:S(2)}, u32[]{:S(2)}) collective-permute-start(bf16[80,2560]{1,0:T(8,128)(2,1)} %get-tuple-element.87), channel_id=1, source_target_pairs={{0,6},{2,4},{4,2},{6,0},{8,14},{10,12},{12,10},{14,8},{1,7},{3,5},... | collective-permute-start | bytes 1228808 | tf_op jit(solution)/shard_map/ppermute | solution.py:222
  24.7 6.8 %collective-permute-done.13.refs_3_ = bf16[80,2688]{1,0:T(8,128)(2,1)S(1)} collective-permute-done((bf16[80,2688]{1,0:T(8,128)(2,1)}, bf16[80,2688]{1,0:T(8,128)(2,1)S(1)}, u32[]{:S(2)}, u32[]{:S(2)}) %collective-permute-start.13) | collective-permute-done | bytes 430112 | tf_op jit(solution)/shard_map/ppermute | solution.py:222
  31.5 4.3 %shard_map.60 = (s16[64,2688]{1,0:T(8,128)(2,1)}, f32[64,2560]{1,0:T(8,128)S(1)}, bf16[320,2560]{1,0:T(8,128)(2,1)S(1)}, bf16[320,2560]{1,0:T(8,128)(2,1)}, bf16...) custom-call(bf16[80,2688]{1,0:T(8,128)(2,1)S(1)} %get-tuple-element., ...), custom_call_target="tpu_custom_call" | custom-call | tf_op jit(solution)/shard_map/pallas_call | solution.py:257
  35.8 1.2 %copy-done.2 = bf16[320,2560]{1,0:T(8,128)(2,1)} copy-done((bf16[320,2560]{1,0:T(8,128)(2,1)}, bf16[320,2560]{1,0:T(8,128)(2,1)S(1)}, u32[]{:S(2)}) %copy-start.2) | copy-done | bytes 1638424
  37.0 0.8 copy-done.11
  37.8 3.1 %collective-permute-start.14 = (s16[64,2688]{1,0:T(8,128)(2,1)}, s16[64,2688]{1,0:T(8,128)(2,1)}, u32[]{:S(2)}, u32[]{:S(2)}) collective-permute-start(s16[64,2688]{1,0:T(8,128)(2,1)} %get-tuple-element.76), channel_id=1, source_target_pairs={{0,8},{2,10},{4,12},{6,14},{8,0},{10,2},{12,4},{14,6},{1,9},{3,11}... | collective-permute-start | bytes 1032200 | tf_op jit(solution)/shard_map/ppermute | solution.py:265
  40.9 0.8 copy-done.15
  41.7 6.5 %collective-permute-done.16.refs_2_ = bf16[80,2560]{1,0:T(8,128)(2,1)S(1)} collective-permute-done((bf16[80,2560]{1,0:T(8,128)(2,1)}, bf16[80,2560]{1,0:T(8,128)(2,1)S(1)}, u32[]{:S(2)}, u32[]{:S(2)}) %collective-permute-start.16) | collective-permute-done | bytes 409632 | tf_op jit(solution)/shard_map/ppermute | solution.py:222
  48.1 0.7 copy-done.17
  48.9 6.4 %collective-permute-done.17.refs_3_ = bf16[80,2560]{1,0:T(8,128)(2,1)S(1)} collective-permute-done((bf16[80,2560]{1,0:T(8,128)(2,1)}, bf16[80,2560]{1,0:T(8,128)(2,1)S(1)}, u32[]{:S(2)}, u32[]{:S(2)}) %collective-permute-start.17) | collective-permute-done | bytes 409632 | tf_op jit(solution)/shard_map/ppermute | solution.py:222
  55.2 0.8 copy-done.19
  56.0 1.0 %copy-done.16 = bf16[80,2560]{1,0:T(8,128)(2,1)S(1)} copy-done((bf16[80,2560]{1,0:T(8,128)(2,1)S(1)}, bf16[80,2560]{1,0:T(8,128)(2,1)}, u32[]{:S(2)}) %copy-start.16) | copy-done | bytes 409624
  57.0 1.0 %copy-done.18 = bf16[80,2560]{1,0:T(8,128)(2,1)S(1)} copy-done((bf16[80,2560]{1,0:T(8,128)(2,1)S(1)}, bf16[80,2560]{1,0:T(8,128)(2,1)}, u32[]{:S(2)}) %copy-start.18) | copy-done | bytes 409624
  58.0 1.0 %copy-done.20 = bf16[80,2560]{1,0:T(8,128)(2,1)S(1)} copy-done((bf16[80,2560]{1,0:T(8,128)(2,1)S(1)}, bf16[80,2560]{1,0:T(8,128)(2,1)}, u32[]{:S(2)}) %copy-start.20) | copy-done | bytes 409624
  59.0 3.1 %shard_map.63 = (s16[64,2688]{1,0:T(8,128)(2,1)}, f32[64,2560]{1,0:T(8,128)S(1)}, bf16[320,2560]{1,0:T(8,128)(2,1)S(1)}, bf16[320,2560]{1,0:T(8,128)(2,1)S(1)}) custom-call(bf16[80,2560]{1,0:T(8,128)(2,1)S(1)} %copy-done.14, bf16[80,2560]{1,0:T(8,128)(2,1)S(1)} %copy-done.16, bf16[80,2560]{1,0:T(8,128)(2,1)S(1)} %copy-done.18, ...), custom_call_target="tpu_custom_call" | custom-call | tf_op jit(solution)/shard_map/pallas_call | solution.py:197
  62.1 0.8 copy-done.7
  63.0 2.0 %collective-permute-start.18 = (s16[64,2688]{1,0:T(8,128)(2,1)}, s16[64,2688]{1,0:T(8,128)(2,1)}, u32[]{:S(2)}, u32[]{:S(2)}) collective-permute-start(s16[64,2688]{1,0:T(8,128)(2,1)} %get-tuple-element.90), channel_id=1, source_target_pairs={{0,8},{2,10},{4,12},{6,14},{8,0},{10,2},{12,4},{14,6},{1,9},{3,11}... | collective-permute-start | bytes 1032200 | tf_op jit(solution)/shard_map/ppermute | solution.py:265
  65.0 1.4 %copy-done.3 = bf16[320,2560]{1,0:T(8,128)(2,1)S(1)} copy-done((bf16[320,2560]{1,0:T(8,128)(2,1)S(1)}, bf16[320,2560]{1,0:T(8,128)(2,1)}, u32[]{:S(2)}) %copy-start.3) | copy-done | bytes 1638424
  66.4 1.4 %copy-done.4 = bf16[320,2560]{1,0:T(8,128)(2,1)S(1)} copy-done((bf16[320,2560]{1,0:T(8,128)(2,1)S(1)}, bf16[320,2560]{1,0:T(8,128)(2,1)}, u32[]{:S(2)}) %copy-start.4) | copy-done | bytes 1638424
  67.8 1.1 %copy-done.12 = f32[64,2560]{1,0:T(8,128)S(1)} copy-done((f32[64,2560]{1,0:T(8,128)S(1)}, f32[64,2560]{1,0:T(8,128)}, u32[]{:S(2)}) %copy-start.12) | copy-done | bytes 655384
  68.9 2.2 %shard_map.61 = (bf16[64,2560]{1,0:T(8,128)(2,1)S(1)}, f32[64,128]{1,0:T(8,128)S(1)}, f32[8,320]{1,0:T(8,128)S(1)}) custom-call(s16[64,2688]{1,0:T(8,128)(2,1)} %collective-permute-done.14.refs_0_, f32[64,2560]{1,0:T(8,128)S(1)} %copy-done.12, bf16[320,2560]{1,0:T(8,128)(2,1)S(1)} %copy-done.3, bf16[320,2560]{1,0:T(8,128)(2,1)S(1)} %copy-done.4, ...), custom_call_target="tpu_custom_call" | custom-call | tf_op jit(solution)/shard_map/pallas_call | solution.py:197
  71.1 9.4 %collective-permute-done.18.refs_0_ = s16[64,2688]{1,0:T(8,128)(2,1)} collective-permute-done((s16[64,2688]{1,0:T(8,128)(2,1)}, s16[64,2688]{1,0:T(8,128)(2,1)}, u32[]{:S(2)}, u32[]{:S(2)}) %collective-permute-start.18) | collective-permute-done | bytes 344096 | tf_op jit(solution)/shard_map/ppermute | solution.py:265
  80.5 2.2 %shard_map.64 = (bf16[64,2560]{1,0:T(8,128)(2,1)S(1)}, f32[8,128]{1,0:T(8,128)S(1)}) custom-call(s16[64,2688]{1,0:T(8,128)(2,1)} %collective-permute-done.18.refs_0_, f32[64,2560]{1,0:T(8,128)S(1)} %copy-done.8, bf16[320,2560]{1,0:T(8,128)(2,1)S(1)} %get-tuple-element.92.refs_2_, bf16[320,2560]{1,0:T(8,128)(2,1)S(1)} %get-tuple-element.93.refs_3_, ...), custom_call_target="tpu_custom_call" | custom-call | tf_op jit(solution)/shard_map/pallas_call | solution.py:197
  82.7 0.7 copy-done.23
  83.4 2.4 %psum.14.refs_0_ = f32[8,128]{1,0:T(8,128)S(1)} all-reduce(f32[8,128]{1,0:T(8,128)S(1)} %get-tuple-element.95), channel_id=1, replica_groups=mesh['groups'=2,'dom'=4,'cls'=2,'coef'=2] {'coef'}, use_global_device_ids=true, to_apply=%region_0.1 | all-reduce | flops 1024 | bytes 8192 | tf_op jit(solution)/shard_map/psum | solution.py:283
  85.9 1.3 %collective-permute-start.19 = (f32[8,128]{1,0:T(8,128)S(1)}, f32[8,128]{1,0:T(8,128)S(1)}, u32[]{:S(2)}, u32[]{:S(2)}) collective-permute-start(f32[8,128]{1,0:T(8,128)S(1)} %psum.14.refs_0_), channel_id=1, source_target_pairs={{2,0},{0,2},{6,4},{4,6},{10,8},{8,10},{14,12},{12,14},{3,1},{1,3},... | collective-permute-start | bytes 12296 | tf_op jit(solution)/shard_map/ppermute | solution.py:286
  87.2 2.2 %collective-permute-start.21 = (f32[8,128]{1,0:T(8,128)S(1)}, f32[8,128]{1,0:T(8,128)S(1)}, u32[]{:S(2)}, u32[]{:S(2)}) collective-permute-start(f32[8,128]{1,0:T(8,128)S(1)} %psum.14.refs_0_), channel_id=1, source_target_pairs={{6,0},{4,2},{2,4},{0,6},{14,8},{12,10},{10,12},{8,14},{7,1},{5,3},... | collective-permute-start | bytes 12296 | tf_op jit(solution)/shard_map/ppermute | solution.py:286
  89.3 0.9 constant_dynamic-slice_fusion.2
  90.3 0.9 constant_dynamic-slice_fusion.3
  91.3 0.3 pad_maximum_fusion.1
  91.6 0.6 slice.16
  92.9 0.3 shard_map.65
  93.1 0.1 conditional.1
  93.3 0.7 copy-done.24
  (38 shorter events, 0.2 us)
Async XLA Ops:
  4.2 0.7 copy-start.25
  4.2 0.7 copy-start.26
  6.7 14.2 %collective-permute-start.11 = (bf16[80,2688]{1,0:T(8,128)(2,1)S(1)}, bf16[80,2688]{1,0:T(8,128)(2,1)S(1)}, u32[]{:S(2)}, u32[]{:S(2)}) collective-permute-start(bf16[80,2688]{1,0:T(8,128)(2,1)S(1)} %get-tuple-element.73), channel_id=1, source_target_pairs={{0,2},{2,0},{4,6},{6,4},{8,10},{10,8},{12,14},{14,12},{1,3},{3,1},... | collective-permute-start | bytes 1290248 | tf_op jit(solution)/shard_map/ppermute | solution.py:222
  9.7 15.0 %collective-permute-start.12 = (bf16[80,2688]{1,0:T(8,128)(2,1)}, bf16[80,2688]{1,0:T(8,128)(2,1)S(1)}, u32[]{:S(2)}, u32[]{:S(2)}) collective-permute-start(bf16[80,2688]{1,0:T(8,128)(2,1)} %get-tuple-element.74), channel_id=1, source_target_pairs={{0,4},{2,6},{4,0},{6,2},{8,12},{10,14},{12,8},{14,10},{1,5},{3,7},... | collective-permute-start | bytes 1290248 | tf_op jit(solution)/shard_map/ppermute | solution.py:222
  11.2 20.2 %collective-permute-start.13 = (bf16[80,2688]{1,0:T(8,128)(2,1)}, bf16[80,2688]{1,0:T(8,128)(2,1)S(1)}, u32[]{:S(2)}, u32[]{:S(2)}) collective-permute-start(bf16[80,2688]{1,0:T(8,128)(2,1)} %get-tuple-element.75), channel_id=1, source_target_pairs={{0,6},{2,4},{4,2},{6,0},{8,14},{10,12},{12,10},{14,8},{1,7},{3,5},... | collective-permute-start | bytes 1290248 | tf_op jit(solution)/shard_map/ppermute | solution.py:222
  13.1 0.8 copy-start.13
  13.8 27.1 %collective-permute-start.15 = (bf16[80,2560]{1,0:T(8,128)(2,1)}, bf16[80,2560]{1,0:T(8,128)(2,1)S(1)}, u32[]{:S(2)}, u32[]{:S(2)}) collective-permute-start(bf16[80,2560]{1,0:T(8,128)(2,1)} %get-tuple-element.85), channel_id=1, source_target_pairs={{0,2},{2,0},{4,6},{6,4},{8,10},{10,8},{12,14},{14,12},{1,3},{3,1},... | collective-permute-start | bytes 1228808 | tf_op jit(solution)/shard_map/ppermute | solution.py:222
  15.7 32.4 %collective-permute-start.16 = (bf16[80,2560]{1,0:T(8,128)(2,1)}, bf16[80,2560]{1,0:T(8,128)(2,1)S(1)}, u32[]{:S(2)}, u32[]{:S(2)}) collective-permute-start(bf16[80,2560]{1,0:T(8,128)(2,1)} %get-tuple-element.86), channel_id=1, source_target_pairs={{0,4},{2,6},{4,0},{6,2},{8,12},{10,14},{12,8},{14,10},{1,5},{3,7},... | collective-permute-start | bytes 1228808 | tf_op jit(solution)/shard_map/ppermute | solution.py:222
  20.9 34.3 %collective-permute-start.17 = (bf16[80,2560]{1,0:T(8,128)(2,1)}, bf16[80,2560]{1,0:T(8,128)(2,1)S(1)}, u32[]{:S(2)}, u32[]{:S(2)}) collective-permute-start(bf16[80,2560]{1,0:T(8,128)(2,1)} %get-tuple-element.87), channel_id=1, source_target_pairs={{0,6},{2,4},{4,2},{6,0},{8,14},{10,12},{12,10},{14,8},{1,7},{3,5},... | collective-permute-start | bytes 1228808 | tf_op jit(solution)/shard_map/ppermute | solution.py:222
  24.7 31.3 %copy-start.14 = (bf16[80,2560]{1,0:T(8,128)(2,1)S(1)}, bf16[80,2560]{1,0:T(8,128)(2,1)}, u32[]{:S(2)}) copy-start(bf16[80,2560]{1,0:T(8,128)(2,1)} %copy-done.13) | copy-start | bytes 1228804
  35.8 1.2 %copy-start.2 = (bf16[320,2560]{1,0:T(8,128)(2,1)}, bf16[320,2560]{1,0:T(8,128)(2,1)S(1)}, u32[]{:S(2)}) copy-start(bf16[320,2560]{1,0:T(8,128)(2,1)S(1)} %get-tuple-element.78.refs_2_) | copy-start | bytes 4915204
  37.0 0.8 copy-start.11
  37.8 27.1 %collective-permute-start.14 = (s16[64,2688]{1,0:T(8,128)(2,1)}, s16[64,2688]{1,0:T(8,128)(2,1)}, u32[]{:S(2)}, u32[]{:S(2)}) collective-permute-start(s16[64,2688]{1,0:T(8,128)(2,1)} %get-tuple-element.76), channel_id=1, source_target_pairs={{0,8},{2,10},{4,12},{6,14},{8,0},{10,2},{12,4},{14,6},{1,9},{3,11}... | collective-permute-start | bytes 1032200 | tf_op jit(solution)/shard_map/ppermute | solution.py:265
  40.9 0.8 copy-start.15
  48.1 0.8 copy-start.17
  55.2 0.8 copy-start.19
  56.0 1.0 %copy-start.16 = (bf16[80,2560]{1,0:T(8,128)(2,1)S(1)}, bf16[80,2560]{1,0:T(8,128)(2,1)}, u32[]{:S(2)}) copy-start(bf16[80,2560]{1,0:T(8,128)(2,1)} %copy-done.15) | copy-start | bytes 1228804
  57.0 1.0 %copy-start.18 = (bf16[80,2560]{1,0:T(8,128)(2,1)S(1)}, bf16[80,2560]{1,0:T(8,128)(2,1)}, u32[]{:S(2)}) copy-start(bf16[80,2560]{1,0:T(8,128)(2,1)} %copy-done.17) | copy-start | bytes 1228804
  58.0 1.0 %copy-start.20 = (bf16[80,2560]{1,0:T(8,128)(2,1)S(1)}, bf16[80,2560]{1,0:T(8,128)(2,1)}, u32[]{:S(2)}) copy-start(bf16[80,2560]{1,0:T(8,128)(2,1)} %copy-done.19) | copy-start | bytes 1228804
  62.1 0.8 copy-start.7
  63.0 17.5 %collective-permute-start.18 = (s16[64,2688]{1,0:T(8,128)(2,1)}, s16[64,2688]{1,0:T(8,128)(2,1)}, u32[]{:S(2)}, u32[]{:S(2)}) collective-permute-start(s16[64,2688]{1,0:T(8,128)(2,1)} %get-tuple-element.90), channel_id=1, source_target_pairs={{0,8},{2,10},{4,12},{6,14},{8,0},{10,2},{12,4},{14,6},{1,9},{3,11}... | collective-permute-start | bytes 1032200 | tf_op jit(solution)/shard_map/ppermute | solution.py:265
  65.0 1.4 %copy-start.3 = (bf16[320,2560]{1,0:T(8,128)(2,1)S(1)}, bf16[320,2560]{1,0:T(8,128)(2,1)}, u32[]{:S(2)}) copy-start(bf16[320,2560]{1,0:T(8,128)(2,1)} %copy-done.2) | copy-start | bytes 4915204
  66.4 1.4 %copy-start.4 = (bf16[320,2560]{1,0:T(8,128)(2,1)S(1)}, bf16[320,2560]{1,0:T(8,128)(2,1)}, u32[]{:S(2)}) copy-start(bf16[320,2560]{1,0:T(8,128)(2,1)} %get-tuple-element.79.refs_3_) | copy-start | bytes 4915204
  67.8 1.1 %copy-start.12 = (f32[64,2560]{1,0:T(8,128)S(1)}, f32[64,2560]{1,0:T(8,128)}, u32[]{:S(2)}) copy-start(f32[64,2560]{1,0:T(8,128)} %copy-done.11) | copy-start | bytes 1966084
  68.9 11.6 %copy-start.8 = (f32[64,2560]{1,0:T(8,128)S(1)}, f32[64,2560]{1,0:T(8,128)}, u32[]{:S(2)}) copy-start(f32[64,2560]{1,0:T(8,128)} %copy-done.7) | copy-start | bytes 1966084
  71.1 11.6 %copy-start.21 = (bf16[64,2560]{1,0:T(8,128)(2,1)}, bf16[64,2560]{1,0:T(8,128)(2,1)S(1)}, u32[]{:S(2)}) copy-start(bf16[64,2560]{1,0:T(8,128)(2,1)S(1)} %get-tuple-element.96) | copy-start | bytes 983044
  82.7 0.7 copy-start.23
  85.9 7.0 %collective-permute-start.19 = (f32[8,128]{1,0:T(8,128)S(1)}, f32[8,128]{1,0:T(8,128)S(1)}, u32[]{:S(2)}, u32[]{:S(2)}) collective-permute-start(f32[8,128]{1,0:T(8,128)S(1)} %psum.14.refs_0_), channel_id=1, source_target_pairs={{2,0},{0,2},{6,4},{4,6},{10,8},{8,10},{14,12},{12,14},{3,1},{1,3},... | collective-permute-start | bytes 12296 | tf_op jit(solution)/shard_map/ppermute | solution.py:286
  87.2 5.7 %collective-permute-start.20 = (f32[8,128]{1,0:T(8,128)S(1)}, f32[8,128]{1,0:T(8,128)S(1)}, u32[]{:S(2)}, u32[]{:S(2)}) collective-permute-start(f32[8,128]{1,0:T(8,128)S(1)} %psum.14.refs_0_), channel_id=1, source_target_pairs={{4,0},{6,2},{0,4},{2,6},{12,8},{14,10},{8,12},{10,14},{5,1},{7,3},... | collective-permute-start | bytes 12296 | tf_op jit(solution)/shard_map/ppermute | solution.py:286
  87.2 5.7 %collective-permute-start.21 = (f32[8,128]{1,0:T(8,128)S(1)}, f32[8,128]{1,0:T(8,128)S(1)}, u32[]{:S(2)}, u32[]{:S(2)}) collective-permute-start(f32[8,128]{1,0:T(8,128)S(1)} %psum.14.refs_0_), channel_id=1, source_target_pairs={{6,0},{4,2},{2,4},{0,6},{14,8},{12,10},{10,12},{8,14},{7,1},{5,3},... | collective-permute-start | bytes 12296 | tf_op jit(solution)/shard_map/ppermute | solution.py:286
  93.3 0.7 copy-start.24
  93.3 0.7 copy-start.27

commit v2 on v1

--- a/solution.py
+++ b/solution.py
@@ -14,8 +14,14 @@
 CAP = 2
 LANES = 128
 BLOCK = 256
-SHARES = (0.5, 0.5)
-PARAMS = pltpu.CompilerParams(vmem_limit_bytes=48 << 20)
+SHARES = (0.3, 0.3, 0.4)
+PIN = 1
+GATE = 0
+HOLD = False
+COST = 5
+FLOWS = (3, 1, 2)
+ROWS = 8
+PARAMS = pltpu.CompilerParams(vmem_limit_bytes=20 << 20)
 NT = (((1,), (1,)), ((), ()))
 f32 = jnp.float32
 bf16 = jnp.bfloat16
@@ -43,12 +49,36 @@
     return jnp.where(rows == slot, 1.0, 0.0).astype(bf16)
 
 
-def pack_first(parts, cap, meta_ref, x_ref, *out_refs):
+def pick_lanes(x_ref, lanes, start, width):
+    return [x_ref[:, pl.ds(first + start, width)] for first in (0, lanes)]
+
+
+def whole(value, by):
+    return jnp.floor((value + 0.5) * (1.0 / by))
+
+
+def pack_first(
+    parts, cap, grid, width, x_ref, label_ref, angle_ref, count_ref, z_ref, column_ref, *refs
+):
+    out_refs, (held_ref, semaphore) = refs[:-2], refs[-2:]
+    n_dom, n_cls, pair = grid
+    copy = pltpu.make_async_copy(x_ref.at[:, :, pl.ds(0, width)], held_ref, semaphore)
+    copy.start()
     slot_ref = out_refs[parts]
-    people = meta_ref.shape[1]
-    width = x_ref.shape[1]
-    meta = meta_ref[...]
-    dest = meta[0:1]
+    people = label_ref.shape[1]
+    owned = CLASSES // (n_dom * n_cls)
+    label = label_ref[...].astype(f32)
+    owner = whole(label, owned)
+    z_of = whole(owner, n_cls)
+    x_of = owner - n_cls * z_of
+    group = whole(z_of, pair)
+    depth = z_of - pair * group - lax.rem(z_ref[0, 0], pair).astype(f32)
+    across = x_of - column_ref[0, 0].astype(f32)
+    depth = jnp.where(depth < 0.0, depth + pair, depth)
+    across = jnp.where(across < 0.0, across + n_cls, across)
+    dest = (depth * n_cls + across).astype(i32)
+    index = group * owned + label - owned * owner
+    angle = angle_ref[...]
     chosen = jnp.where(lax.broadcasted_iota(i32, (16, people), 0) == dest, 1.0, 0.0)
     before = jnp.where(
         lax.broadcasted_iota(i32, (people, people), 0) < lax.broadcasted_iota(i32, (people, people), 1), 1.0, 0.0
@@ -58,27 +88,33 @@
     over = jnp.max(jnp.where(rank >= cap, 1.0, 0.0))
     slot = jnp.where(rank < cap, dest * cap + rank, -1)
     slot_ref[...] = jnp.broadcast_to(jnp.where(rank < cap, dest * LANES + rank, -1), slot_ref.shape)
-    half = lax.shift_right_logical(meta[2:3], 1)
+    half = lax.shift_right_logical(angle, 1)
     rows = lax.broadcasted_iota(i32, (LANES, people), 0)
-    details = jnp.where(rows == 0, meta[1:2], 0)
-    details = jnp.where(rows == 1, half, details)
-    details = jnp.where(rows == 2, meta[2:3] - 2 * half, details)
-    details = jnp.where(rows == 3, meta[3:4], details)
-    details = details.astype(f32).astype(bf16)
+    details = jnp.where(rows == 0, index, 0.0)
+    details = jnp.where(rows == 1, half.astype(f32), details)
+    details = jnp.where(rows == 2, (angle - 2 * half).astype(f32), details)
+    details = jnp.where(rows == 3, count_ref[...].astype(f32), details)
+    details = details.astype(bf16)
     lane = lax.broadcasted_iota(i32, (cap, LANES), 1)
+    copy.wait()
+    real, imag = held_ref[:, 0, :], held_ref[:, 1, :]
     for part in range(parts):
         place = place_of(slot - part * cap, cap)
-        out_refs[part][:, :width] = matmul(place, x_ref[...]).astype(bf16)
+        out_refs[part][:, :width] = matmul(place, real).astype(bf16)
+        out_refs[part][:, width : 2 * width] = matmul(place, imag).astype(bf16)
         block = jnp.where(lane == 4, over, matmul(place, details, NT))
-        out_refs[part][:, width:] = block.astype(bf16)
-
-
-def pack_next(parts, cap, slot_ref, x_ref, *out_refs):
+        out_refs[part][:, 2 * width :] = block.astype(bf16)
+
+
+def pack_next(parts, cap, lanes, start, width, slot_ref, x_ref, *out_refs):
+    real, imag = pick_lanes(x_ref, lanes, start, width)
     slot = slot_ref[0:1]
     dest = lax.shift_right_arithmetic(slot, 7)
     slot = jnp.where(slot >= 0, dest * cap + (slot - dest * LANES), -1)
     for part in range(parts):
-        out_refs[part][...] = matmul(place_of(slot - part * cap, cap), x_ref[...]).astype(bf16)
+        place = place_of(slot - part * cap, cap)
+        out_refs[part][:, :width] = matmul(place, real).astype(bf16)
+        out_refs[part][:, width:] = matmul(place, imag).astype(bf16)
 
 
 def align(parts, cap, subs, nfreq, first, freqs, start, *refs):
@@ -87,8 +123,8 @@
     if first:
         core_ref, code_ref, sums_ref, high_ref, mid_ref, cos_ref, sin_ref, hot_ref, info_ref = refs
         core = core_ref[0, 0]
-        details = jnp.concatenate([ref[:, 2 * width :] for ref in taken], axis=0)
-        columns = details.astype(f32)
+        columns = jnp.concatenate([ref[:, 2 * width :].astype(f32) for ref in taken], axis=0)
+        details = columns.astype(bf16)
         angle = 2.0 * columns[:, 1:2] + columns[:, 2:3]
         rows = parts * cap
         lane = lax.broadcasted_iota(i32, (rows, cos_ref.shape[1]), 1)
@@ -127,8 +163,8 @@
         at_im = pl.ds(width + block * BLOCK, BLOCK)
         spread = jnp.where(inside & (row == lane_freq + (start + block * (BLOCK // NQ))), 1.0, 0.0).astype(bf16)
         cosine, sine = matmul(cosines, spread), matmul(sines, spread)
-        real = jnp.concatenate([ref[:, at] for ref in taken], axis=0).astype(f32)
-        imag = jnp.concatenate([ref[:, at_im] for ref in taken], axis=0).astype(f32)
+        real = jnp.concatenate([ref[:, at].astype(f32) for ref in taken], axis=0)
+        imag = jnp.concatenate([ref[:, at_im].astype(f32) for ref in taken], axis=0)
         for here, value in ((at, real * cosine - imag * sine), (at_im, real * sine + imag * cosine)):
             high, mid = split(value)
             high_ref[:, here] = high
@@ -192,12 +228,27 @@
     out_ref[...] = total[0:1] * (1.0 / math.sqrt(2.0 * NK * NQ))
 
 
-def call(kernel, outs, *args):
-    shapes = [jax.ShapeDtypeStruct(shape, dtype) for shape, dtype in outs]
-    return pl.pallas_call(kernel, out_shape=shapes, compiler_params=PARAMS)(*args)
-
-
-def exchange(cap, particles, meta, square, n_dom, n_cls, pair):
+def call(kernel, outs, *args, work=1, scalars=0, pin=False, far=0, scratch=()):
+    shapes = [
+        (pltpu.HBM if pin and math.prod(shape) > 1 << 15 else jax.ShapeDtypeStruct)(shape, dtype) for shape, dtype in outs
+    ]
+    specs = [pl.BlockSpec(memory_space=pl.ANY)] * far
+    specs += [pl.BlockSpec(memory_space=pltpu.VMEM)] * (len(args) - scalars - far)
+    specs += [pl.BlockSpec(memory_space=pltpu.SMEM)] * scalars
+    places = [pl.BlockSpec(memory_space=pltpu.VMEM)] * len(outs)
+    cost = pl.CostEstimate(flops=int(work * COST * 10**9), bytes_accessed=0, transcendentals=0) if COST else None
+    return pl.pallas_call(
+        kernel,
+        in_specs=specs,
+        out_specs=places,
+        out_shape=shapes,
+        scratch_shapes=scratch,
+        cost_estimate=cost,
+        compiler_params=PARAMS,
+    )(*args)
+
+
+def exchange(cap, particles, label, angles, counts, square, n_dom, n_cls, pair):
     people, _, width = particles.shape
     axes = ("dom", "cls")
     parts = pair * n_cls
@@ -219,26 +270,48 @@
         return [(z * n_cls + x, ((z // pair + turn) % groups * pair + z % pair) * n_cls + x) for z, x in devices]
 
     def deliver(packed):
-        sent = [lax.ppermute(packed[part], axes, forward(part)) for part in range(1, parts)]
-        return [packed[0], *sent]
+        taken = {0: packed[0]}
+        for part in FLOWS if parts == 4 else range(1, parts):
+            taken[part] = lax.ppermute(packed[part], axes, forward(part))
+        return [taken[part] for part in range(parts)]
 
     lanes = -(-3 * nfreq // LANES) * LANES
     starts = [sum(sizes[:i]) for i in range(len(sizes))]
     core = lax.axis_index("coef").reshape(1, 1).astype(i32)
     arrived = []
-    slot = None
+    rest = None
     for number, (start, freqs) in enumerate(zip(starts, sizes)):
-        x = particles[:, :, start * NQ : (start + freqs) * NQ].reshape(people, 2 * freqs * NQ)
         if number == 0:
+            size = freqs * NQ
             *packed, slot = call(
-                functools.partial(pack_first, parts, cap),
-                [((cap, 2 * freqs * NQ + LANES), bf16)] * parts + [((8, people), i32)],
-                meta,
-                x,
+                functools.partial(pack_first, parts, cap, (n_dom, n_cls, pair), size),
+                [((cap, 2 * size + LANES), bf16)] * parts + [((8, people), i32)],
+                particles,
+                label,
+                angles[None],
+                counts[None],
+                lax.axis_index("dom").reshape(1, 1).astype(i32),
+                lax.axis_index("cls").reshape(1, 1).astype(i32),
+                scalars=2,
+                far=1,
+                work=3,
+                scratch=[pltpu.VMEM((people, 2, size), bf16), pltpu.SemaphoreType.DMA],
+                pin=PIN >= 2,
             )
         else:
+            if number == 1:
+                rest = particles
+                if HOLD:
+                    rest, slot = lax.optimization_barrier((particles, slot))
+                rest = rest.reshape(people, 2 * width)
+            if GATE:
+                slot, arrived[-1][GATE] = lax.optimization_barrier((slot, arrived[-1][GATE]))
             packed = call(
-                functools.partial(pack_next, parts, cap), [((cap, 2 * freqs * NQ), bf16)] * parts, slot, x
+                functools.partial(pack_next, parts, cap, width, start * NQ, freqs * NQ),
+                [((cap, 2 * freqs * NQ), bf16)] * parts,
+                slot,
+                rest,
+                pin=PIN >= 2,
             )
         arrived.append(deliver(packed))
     aligned = []
@@ -253,15 +326,13 @@
         ]
         if number == 0:
             more = [((rows, lanes), bf16)] * 2 + [((2, subs, rows), bf16), ((subs, LANES), f32)]
-            specs = [pl.BlockSpec(memory_space=pltpu.VMEM)] * parts + [pl.BlockSpec(memory_space=pltpu.SMEM)]
-            code, sums, high, mid, cosines, sines, hot, info = pl.pallas_call(
-                kernel,
-                in_specs=specs,
-                out_shape=[jax.ShapeDtypeStruct(*out) for out in outs + more],
-                compiler_params=PARAMS,
-            )(*arrived[0], core)
+            code, sums, high, mid, cosines, sines, hot, info = call(
+                kernel, outs + more, *arrived[0], core, scalars=1, work=4, pin=PIN >= 1
+            )
         else:
-            code, sums, high, mid = call(kernel, outs, *arrived[number], cosines, sines, hot)
+            code, sums, high, mid = call(
+                kernel, outs, *arrived[number], cosines, sines, hot, work=3, pin=PIN >= 1
+            )
         codes = [lax.ppermute(code, axes, across(turn)) for turn in range(1, groups)]
         aligned.append((codes, sums, high, mid))
     means = []
@@ -280,7 +351,6 @@
         else:
             mean, gain = call(kernel, outs, *args, gain)
         means.append(mean)
-    gain = lax.psum(gain, "coef")
     returned = [gain]
     for part in range(1, parts):
         returned.append(lax.ppermute(gain, axes, [(b, a) for a, b in forward(part)]))
@@ -289,36 +359,35 @@
         lax.dynamic_slice_in_dim(mean, square * owned, owned).reshape(owned, 2, -1) for mean in means
     ]
     averages = jnp.concatenate(mine, axis=2)
-    return averages, gains.reshape(people), info[0, 2] > 0.0
+    return averages, gains, info[0, 2] > 0.0
 
 
 def shards(particles, classes, angles, counts):
     n_dom = lax.axis_size("dom")
     n_cls = lax.axis_size("cls")
     pair = 2 if n_dom % 2 == 0 else 1
-    z, x = lax.axis_index("dom"), lax.axis_index("cls")
+    z = lax.axis_index("dom")
     people = particles.shape[0]
     owned = CLASSES // (n_dom * n_cls)
     subs = n_dom // pair * owned
     parts = pair * n_cls
     label = classes.reshape(1, people)
-    owner = label // owned
-    z_of, x_of = owner // n_cls, owner % n_cls
-    dest = (z_of % pair + pair - z % pair) % pair * n_cls + (x_of + n_cls - x) % n_cls
-    index = z_of // pair * owned + label % owned
-    meta = jnp.concatenate([dest, index, angles[None], counts[None], jnp.zeros((4, people), i32)], axis=0)
     mean_rows = people / parts
-    most = min(CAP * subs, people + 15) // 16 * 16
-    cap = min(most, -(-int(mean_rows + 3.2 * math.sqrt(mean_rows)) // 16) * 16)
+    most = min(CAP * subs, people + ROWS - 1) // ROWS * ROWS
+    cap = min(most, -(-int(mean_rows + 2.0 * math.sqrt(mean_rows)) // ROWS) * ROWS)
     run = functools.partial(exchange, n_dom=n_dom, n_cls=n_cls, pair=pair)
-    averages, gains, over = run(cap, particles, meta, z // pair)
-    if cap == most:
-        return averages, gains
-    return lax.cond(
-        over,
-        lambda: run(most, particles, meta, z // pair)[:2],
-        lambda: (averages, gains),
-    )
+    averages, gains, over = run(cap, particles, label, angles, counts, z // pair)
+    if cap < most:
+        averages, gains = lax.cond(
+            over,
+            lambda: run(most, particles, label, angles, counts, z // pair)[:2],
+            lambda: (averages, gains),
+        )
+    n_coef = lax.axis_size("coef")
+    total = gains
+    for turn in range(1, n_coef):
+        total = total + lax.ppermute(gains, "coef", [(i, (i + turn) % n_coef) for i in range(n_coef)])
+    return averages, total.reshape(people)
 
 
 def solution(mesh):

time: 94.5 us -> 78.2 us (0.83)
  local copies, waits for them, and re-layouts: 20.5 us -> 7.66 us
  waiting for transfers between devices: 32.6 us -> 21.9 us
  starting transfers between devices: 20.3 us -> 26.6 us
  Pallas kernels: 15.6 us -> 19 us
  blocking collectives: 2.44 us -> 0 us
    ppermute x6 -> x10, waiting for transfers between devices: 23.2 us -> 10.9 us  [the longest x9 9.81 us: deliver(): taken[part] = lax.ppermute(packed[part], axes, forward(part))]
    unnamed x44 -> x53, local copies, waits for them, and re-layouts: 15 us -> 5.31 us
    ppermute x2 -> x3, starting transfers between devices: 5.05 us -> 8.54 us  [exchange(): lax.ppermute(code, axes, across(turn))]
    pallas_call x7 -> x10, Pallas kernels: 15.6 us -> 19 us  [call(): pl.pallas_call(kernel, in_specs=specs, out_specs=places, out_shape=shapes...]
    ppermute x6 -> x10, starting transfers between devices: 11.8 us -> 14.6 us  [the longest x9 14.5 us: deliver(): taken[part] = lax.ppermute(packed[part], axes, forward(part))]
    slice x2 -> x1, local copies, waits for them, and re-layouts: 3.43 us -> 0.65 us  [exchange(): return (averages, gains, info[0, 2] > 0.0)]
    psum x1 -> x0, blocking collectives: 2.44 us -> none  [exchange(): gain = lax.psum(gain, 'coef')]
    ppermute x3, waiting for transfers between devices: 0.01 us -> 2.2 us  [exchange(): lax.ppermute(gain, axes, [(b, a) for a, b in forward(part)])]
  transfers between devices with their start and end apart: 11 -> 16, of which waited for: 5 -> 9; matrix products, arithmetic and copies ran while one was open for 3% -> 4% of each run, Pallas kernels for 12% -> 17%
where the time goes in v2:
time: 78.2 us; the launch traced here: 77.8 us
  starting transfers between devices  26.6 us (34%)
  waiting for transfers between devices  21.9 us (28%)
  Pallas kernels  19 us (24%)
  local copies, waits for them, and re-layouts  7.66 us (10%)
  between operations  1.59 us (2%)
  other arithmetic  0.85 us (1%)
    pallas_call x10, Pallas kernels, call(): pl.pallas_call(kernel, in_specs=specs, out_specs=places, out_shape=shapes...  19 us
    ppermute x9, starting transfers between devices, deliver(): taken[part] = lax.ppermute(packed[part], axes, forward(part))  14.5 us
    ppermute x9, waiting for transfers between devices, deliver(): taken[part] = lax.ppermute(packed[part], axes, forward(part))  9.81 us
    ppermute x3, waiting for transfers between devices, exchange(): lax.ppermute(code, axes, across(turn))  8.74 us
    ppermute x3, starting transfers between devices, exchange(): lax.ppermute(code, axes, across(turn))  8.54 us
    unnamed x53, local copies, waits for them, and re-layouts  5.31 us
    ppermute x3, starting transfers between devices, exchange(): lax.ppermute(gain, axes, [(b, a) for a, b in forward(part)])  3.49 us
    ppermute x3, waiting for transfers between devices, exchange(): lax.ppermute(gain, axes, [(b, a) for a, b in forward(part)])  2.2 us
  transfers between devices with their start and end apart: 16, of which 9 were waited for; matrix products, arithmetic and copies ran while one was open for 4% of the time, Pallas kernels for 17%

profile of v2, /device:TPU:0, one launch (start us, length us, event | category | flops | bytes accessed | tf_op | source)
XLA Modules:
  0.0 77.8 jit_solution(2553336321398538437)
XLA Ops:
  0.6 4.3 %shard_map.59 = (bf16[72,1664]{1,0:T(8,128)(2,1)S(1)}, bf16[72,1664]{1,0:T(8,128)(2,1)}, bf16[72,1664]{1,0:T(8,128)(2,1)S(1)}, bf16[72,1664]{1,0:T(8,128)(2,1)S(1)}, s32[8,224]{1,0:T(8,128)S(1)}) custom-call(bf16[224,2,2560]{2,1,0:T(2,128)(2,1)} %x_ref.1, s32[1,224]{1,0:T(1,128)} %bitcast.24, s32[1,224]{1,0:T(1,128)} %bitcast.26, s32[1,224]{1,0:T(1,128)} %bitcast.28, ...), custom_call_target="tpu_custom_call" | custom-call | flops 15000000512 | tf_op jit(solution)/shard_map/pallas_call | solution.py:240
  5.0 0.7 copy-done.32
  5.7 2.9 %collective-permute-start.15 = (bf16[72,1664]{1,0:T(8,128)(2,1)}, bf16[72,1664]{1,0:T(8,128)(2,1)S(1)}, u32[]{:S(2)}, u32[]{:S(2)}) collective-permute-start(bf16[72,1664]{1,0:T(8,128)(2,1)} %get-tuple-element.96), channel_id=1, source_target_pairs={{0,2},{2,0},{4,6},{6,4},{8,10},{10,8},{12,14},{14,12},{1,3},{3,1},... | collective-permute-start | bytes 718856 | tf_op jit(solution)/shard_map/ppermute | solution.py:275
  8.6 1.6 %collective-permute-start.16 = (bf16[72,1664]{1,0:T(8,128)(2,1)S(1)}, bf16[72,1664]{1,0:T(8,128)(2,1)S(1)}, u32[]{:S(2)}, u32[]{:S(2)}) collective-permute-start(bf16[72,1664]{1,0:T(8,128)(2,1)S(1)} %get-tuple-element.97), channel_id=1, source_target_pairs={{0,4},{2,6},{4,0},{6,2},{8,12},{10,14},{12,8},{14,10},{1,5},{3,7},... | collective-permute-start | bytes 718856 | tf_op jit(solution)/shard_map/ppermute | solution.py:275
  10.2 0.3 copy.7
  10.6 1.2 %shard_map.62 = (bf16[72,1536]{1,0:T(8,128)(2,1)S(1)}, bf16[72,1536]{1,0:T(8,128)(2,1)}, bf16[72,1536]{1,0:T(8,128)(2,1)}, bf16[72,1536]{1,0:T(8,128)(2,1)S(1)}) custom-call(s32[8,224]{1,0:T(8,128)S(1)} %get-tuple-element.107.slot_ref, bf16[224,5120]{1,0:T(8,128)(2,1)S(1)} %bitcast.17), custom_call_target="tpu_custom_call" | custom-call | flops 5000000000 | tf_op jit(solution)/shard_map/pallas_call | solution.py:240
  11.8 0.7 copy-done.2
  12.5 0.7 copy-done.24
  13.1 1.9 %collective-permute-start.19 = (bf16[72,1536]{1,0:T(8,128)(2,1)}, bf16[72,1536]{1,0:T(8,128)(2,1)}, u32[]{:S(2)}, u32[]{:S(2)}) collective-permute-start(bf16[72,1536]{1,0:T(8,128)(2,1)} %get-tuple-element.109), channel_id=1, source_target_pairs={{0,2},{2,0},{4,6},{6,4},{8,10},{10,8},{12,14},{14,12},{1,3},{3,1},... | collective-permute-start | bytes 663560 | tf_op jit(solution)/shard_map/ppermute | solution.py:275
  15.0 1.6 %collective-permute-start.20 = (bf16[72,1536]{1,0:T(8,128)(2,1)}, bf16[72,1536]{1,0:T(8,128)(2,1)}, u32[]{:S(2)}, u32[]{:S(2)}) collective-permute-start(bf16[72,1536]{1,0:T(8,128)(2,1)} %get-tuple-element.110), channel_id=1, source_target_pairs={{0,4},{2,6},{4,0},{6,2},{8,12},{10,14},{12,8},{14,10},{1,5},{3,7},... | collective-permute-start | bytes 663560 | tf_op jit(solution)/shard_map/ppermute | solution.py:275
  16.6 0.7 shard_map.65
  17.4 0.2 copy-done.3
  17.6 0.4 collective-permute-start.21
  17.9 1.6 %collective-permute-start.23 = (bf16[72,2048]{1,0:T(8,128)(2,1)S(1)}, bf16[72,2048]{1,0:T(8,128)(2,1)S(1)}, u32[]{:S(2)}, u32[]{:S(2)}) collective-permute-start(bf16[72,2048]{1,0:T(8,128)(2,1)S(1)} %get-tuple-element.121), channel_id=1, source_target_pairs={{0,2},{2,0},{4,6},{6,4},{8,10},{10,8},{12,14},{14,12},{1,3},{3,1},... | collective-permute-start | bytes 884744 | tf_op jit(solution)/shard_map/ppermute | solution.py:275
  19.5 2.6 %collective-permute-done.17.refs_3_ = bf16[72,1664]{1,0:T(8,128)(2,1)S(1)} collective-permute-done((bf16[72,1664]{1,0:T(8,128)(2,1)S(1)}, bf16[72,1664]{1,0:T(8,128)(2,1)S(1)}, u32[]{:S(2)}, u32[]{:S(2)}) %collective-permute-start.17) | collective-permute-done | bytes 239648 | tf_op jit(solution)/shard_map/ppermute | solution.py:275
  22.1 2.1 %collective-permute-start.24 = (bf16[72,2048]{1,0:T(8,128)(2,1)S(1)}, bf16[72,2048]{1,0:T(8,128)(2,1)S(1)}, u32[]{:S(2)}, u32[]{:S(2)}) collective-permute-start(bf16[72,2048]{1,0:T(8,128)(2,1)S(1)} %get-tuple-element.122), channel_id=1, source_target_pairs={{0,4},{2,6},{4,0},{6,2},{8,12},{10,14},{12,8},{14,10},{1,5},{3,7},... | collective-permute-start | bytes 884744 | tf_op jit(solution)/shard_map/ppermute | solution.py:275
  24.1 3.2 %shard_map.60 = (s16[64,1664]{1,0:T(8,128)(2,1)}, f32[64,1536]{1,0:T(8,128)}, bf16[288,1536]{1,0:T(8,128)(2,1)}, bf16[288,1536]{1,0:T(8,128)(2,1)}, bf16[288,128...) custom-call(bf16[72,1664]{1,0:T(8,128)(2,1)S(1)} %copy-done.33, ...), custom_call_target="tpu_custom_call" | custom-call | flops 20000000000 | tf_op jit(solution)/shard_map/pallas_call | solution.py:240
  27.4 2.5 %collective-permute-start.25 = (bf16[72,2048]{1,0:T(8,128)(2,1)S(1)}, bf16[72,2048]{1,0:T(8,128)(2,1)S(1)}, u32[]{:S(2)}, u32[]{:S(2)}) collective-permute-start(bf16[72,2048]{1,0:T(8,128)(2,1)S(1)} %get-tuple-element.123), channel_id=1, source_target_pairs={{0,6},{2,4},{4,2},{6,0},{8,14},{10,12},{12,10},{14,8},{1,7},{3,5},... | collective-permute-start | bytes 884744 | tf_op jit(solution)/shard_map/ppermute | solution.py:275
  29.9 2.6 %collective-permute-start.18 = (s16[64,1664]{1,0:T(8,128)(2,1)}, s16[64,1664]{1,0:T(8,128)(2,1)S(1)}, u32[]{:S(2)}, u32[]{:S(2)}) collective-permute-start(s16[64,1664]{1,0:T(8,128)(2,1)} %get-tuple-element.99), channel_id=1, source_target_pairs={{0,8},{2,10},{4,12},{6,14},{8,0},{10,2},{12,4},{14,6},{1,9},{3,11}... | collective-permute-start | bytes 638984 | tf_op jit(solution)/shard_map/ppermute | solution.py:336
  32.5 1.4 %collective-permute-done.21.refs_3_ = bf16[72,1536]{1,0:T(8,128)(2,1)S(1)} collective-permute-done((bf16[72,1536]{1,0:T(8,128)(2,1)S(1)}, bf16[72,1536]{1,0:T(8,128)(2,1)S(1)}, u32[]{:S(2)}, u32[]{:S(2)}) %collective-permute-start.21) | collective-permute-done | bytes 221216 | tf_op jit(solution)/shard_map/ppermute | solution.py:275
  33.9 0.9 %copy-done.28 = bf16[2,64,288]{2,1,0:T(8,128)(2,1)S(1)} copy-done((bf16[2,64,288]{2,1,0:T(8,128)(2,1)S(1)}, bf16[2,64,288]{2,1,0:T(8,128)(2,1)}, u32[]{:S(2)}) %copy-start.28) | copy-done | bytes 73752
  34.8 0.9 %copy-done.38 = bf16[288,128]{1,0:T(8,128)(2,1)S(1)} copy-done((bf16[288,128]{1,0:T(8,128)(2,1)S(1)}, bf16[288,128]{1,0:T(8,128)(2,1)}, u32[]{:S(2)}) %copy-start.38) | copy-done | bytes 73752
  35.6 0.9 %copy-done.39 = bf16[288,128]{1,0:T(8,128)(2,1)S(1)} copy-done((bf16[288,128]{1,0:T(8,128)(2,1)S(1)}, bf16[288,128]{1,0:T(8,128)(2,1)}, u32[]{:S(2)}) %copy-start.39) | copy-done | bytes 73752
  36.5 3.6 %shard_map.63 = (s16[64,1664]{1,0:T(8,128)(2,1)}, f32[64,1536]{1,0:T(8,128)}, bf16[288,1536]{1,0:T(8,128)(2,1)}, bf16[288,1536]{1,0:T(8,128)(2,1)}) custom-call(bf16[72,1536]{1,0:T(8,128)(2,1)S(1)} %copy-done.25, bf16[72,1536]{1,0:T(8,128)(2,1)} %collective-permute-done.19.refs_1_, bf16[72,1536]{1,0:T(8,128)(2,1)} %collective-permute-done.20.refs_2_, ...), custom_call_target="tpu_custom_call" | custom-call | flops 15000000512 | tf_op jit(solution)/shard_map/pallas_call | solution.py:240
  40.1 4.3 %collective-permute-start.22 = (s16[64,1664]{1,0:T(8,128)(2,1)}, s16[64,1664]{1,0:T(8,128)(2,1)S(1)}, u32[]{:S(2)}, u32[]{:S(2)}) collective-permute-start(s16[64,1664]{1,0:T(8,128)(2,1)} %get-tuple-element.114), channel_id=1, source_target_pairs={{0,8},{2,10},{4,12},{6,14},{8,0},{10,2},{12,4},{14,6},{1,9},{3,11}... | collective-permute-start | bytes 638984 | tf_op jit(solution)/shard_map/ppermute | solution.py:336
  44.5 0.8 %collective-permute-done.24.refs_2_ = bf16[72,2048]{1,0:T(8,128)(2,1)S(1)} collective-permute-done((bf16[72,2048]{1,0:T(8,128)(2,1)S(1)}, bf16[72,2048]{1,0:T(8,128)(2,1)S(1)}, u32[]{:S(2)}, u32[]{:S(2)}) %collective-permute-start.24) | collective-permute-done | bytes 294944 | tf_op jit(solution)/shard_map/ppermute | solution.py:275
  45.3 5.0 %collective-permute-done.25.refs_3_ = bf16[72,2048]{1,0:T(8,128)(2,1)S(1)} collective-permute-done((bf16[72,2048]{1,0:T(8,128)(2,1)S(1)}, bf16[72,2048]{1,0:T(8,128)(2,1)S(1)}, u32[]{:S(2)}, u32[]{:S(2)}) %collective-permute-start.25) | collective-permute-done | bytes 294944 | tf_op jit(solution)/shard_map/ppermute | solution.py:275
  50.3 3.2 %shard_map.66 = (s16[64,2176]{1,0:T(8,128)(2,1)}, f32[64,2048]{1,0:T(8,128)}, bf16[288,2048]{1,0:T(8,128)(2,1)}, bf16[288,2048]{1,0:T(8,128)(2,1)}) custom-call(bf16[72,2048]{1,0:T(8,128)(2,1)S(1)} %get-tuple-element.120.refs_0_, bf16[72,2048]{1,0:T(8,128)(2,1)S(1)} %collective-permute-done.23.refs_1_, bf16[72,2048]{1,0:T(8,128)(2,1)S(1)} %collective-permute-done.24.refs_2_, ...), custom_call_target="tpu_custom_call" | custom-call | flops 15000000512 | tf_op jit(solution)/shard_map/pallas_call | solution.py:240
  53.5 1.6 %collective-permute-start.26 = (s16[64,2176]{1,0:T(8,128)(2,1)}, s16[64,2176]{1,0:T(8,128)(2,1)S(1)}, u32[]{:S(2)}, u32[]{:S(2)}) collective-permute-start(s16[64,2176]{1,0:T(8,128)(2,1)} %get-tuple-element.124), channel_id=1, source_target_pairs={{0,8},{2,10},{4,12},{6,14},{8,0},{10,2},{12,4},{14,6},{1,9},{3,11}... | collective-permute-start | bytes 835592 | tf_op jit(solution)/shard_map/ppermute | solution.py:336
  55.1 0.7 shard_map.61
  55.9 0.8 %collective-permute-done.22.refs_0_ = s16[64,1664]{1,0:T(8,128)(2,1)S(1)} collective-permute-done((s16[64,1664]{1,0:T(8,128)(2,1)}, s16[64,1664]{1,0:T(8,128)(2,1)S(1)}, u32[]{:S(2)}, u32[]{:S(2)}) %collective-permute-start.22) | collective-permute-done | bytes 213024 | tf_op jit(solution)/shard_map/ppermute | solution.py:336
  56.7 0.8 shard_map.64
  57.5 0.7 slice.3
  58.8 0.7 constant_dynamic-slice_fusion.4
  59.5 0.9 %reshape.60 = bf16[32,2,768]{2,1,0:T(2,128)(2,1)S(1)} reshape(bf16[32,1536]{1,0:T(8,128)(2,1)} %get-tuple-element.136) | data formatting | bytes 196608 | tf_op jit(solution)/shard_map/reshape | solution.py:359
  60.4 7.9 %collective-permute-done.26.refs_0_ = s16[64,2176]{1,0:T(8,128)(2,1)S(1)} collective-permute-done((s16[64,2176]{1,0:T(8,128)(2,1)}, s16[64,2176]{1,0:T(8,128)(2,1)S(1)}, u32[]{:S(2)}, u32[]{:S(2)}) %collective-permute-start.26) | collective-permute-done | bytes 278560 | tf_op jit(solution)/shard_map/ppermute | solution.py:336
  68.4 1.0 %shard_map.67 = (bf16[64,2048]{1,0:T(8,128)(2,1)S(1)}, f32[8,128]{1,0:T(8,128)S(1)}) custom-call(s16[64,2176]{1,0:T(8,128)(2,1)S(1)} %collective-permute-done.26.refs_0_, f32[64,2048]{1,0:T(8,128)S(1)} %copy-done.17, bf16[288,2048]{1,0:T(8,128)(2,1)S(1)} %copy-done.10, bf16[288,2048]{1,0:T(8,128)(2,1)S(1)} %copy-done.11, bf16[2,64,288]{2,1,0:T(8,128)(2,1)S(1)} %copy-done.29, ...), custom_call_target="tpu_custom_call" | custom-call | flops 5000000000 | tf_op jit(solution)/shard_map/pallas_call | solution.py:240
  69.4 2.5 %collective-permute-start.28 = (f32[8,128]{1,0:T(8,128)S(1)}, f32[8,128]{1,0:T(8,128)S(1)}, u32[]{:S(2)}, u32[]{:S(2)}) collective-permute-start(f32[8,128]{1,0:T(8,128)S(1)} %get-tuple-element.130.refs_0_), channel_id=1, source_target_pairs={{4,0},{6,2},{0,4},{2,6},{12,8},{14,10},{8,12},{10,14},{5,1},{7,3},... | collective-permute-start | bytes 12296 | tf_op jit(solution)/shard_map/ppermute | solution.py:356
  71.9 1.0 %collective-permute-start.27 = (f32[8,128]{1,0:T(8,128)S(1)}, f32[8,128]{1,0:T(8,128)S(1)}, u32[]{:S(2)}, u32[]{:S(2)}) collective-permute-start(f32[8,128]{1,0:T(8,128)S(1)} %get-tuple-element.130.refs_0_), channel_id=1, source_target_pairs={{2,0},{0,2},{6,4},{4,6},{10,8},{8,10},{14,12},{12,14},{3,1},{1,3},... | collective-permute-start | bytes 12296 | tf_op jit(solution)/shard_map/ppermute | solution.py:356
  72.9 0.1 reshape.63
  73.0 0.3 pad_maximum_fusion.1
  73.3 0.6 collective-permute-done.29.refs_3_
  73.9 1.6 %collective-permute-done.27.refs_1_ = f32[8,128]{1,0:T(8,128)S(1)} collective-permute-done((f32[8,128]{1,0:T(8,128)S(1)}, f32[8,128]{1,0:T(8,128)S(1)}, u32[]{:S(2)}, u32[]{:S(2)}) %collective-permute-start.27) | collective-permute-done | bytes 4128 | tf_op jit(solution)/shard_map/ppermute | solution.py:356
  75.5 0.3 shard_map.68
  75.8 0.2 conditional.1
  76.1 0.1 collective-permute-start.30
  76.1 1.1 %collective-permute-done.30 = f32[1,224]{1,0:T(1,128)S(1)} collective-permute-done((f32[1,224]{1,0:T(1,128)S(1)}, f32[1,224]{1,0:T(1,128)S(1)}, u32[]{:S(2)}, u32[]{:S(2)}) %collective-permute-start.30) | collective-permute-done | bytes 928 | tf_op jit(solution)/shard_map/ppermute | solution.py:389
  77.3 0.6 add.16
  (56 shorter events, 0.2 us)
Async XLA Ops:
  0.6 9.6 %copy-start.41 = (bf16[224,2,2560]{2,1,0:T(2,128)(2,1)S(1)}, bf16[224,2,2560]{2,1,0:T(2,128)(2,1)}, u32[]{:S(2)}) copy-start(bf16[224,2,2560]{2,1,0:T(2,128)(2,1)} %x_ref.1) | copy-start | bytes 6881284
  5.0 0.7 copy-start.32
  5.7 11.7 %collective-permute-start.15 = (bf16[72,1664]{1,0:T(8,128)(2,1)}, bf16[72,1664]{1,0:T(8,128)(2,1)S(1)}, u32[]{:S(2)}, u32[]{:S(2)}) collective-permute-start(bf16[72,1664]{1,0:T(8,128)(2,1)} %get-tuple-element.96), channel_id=1, source_target_pairs={{0,2},{2,0},{4,6},{6,4},{8,10},{10,8},{12,14},{14,12},{1,3},{3,1},... | collective-permute-start | bytes 718856 | tf_op jit(solution)/shard_map/ppermute | solution.py:275
  8.6 9.3 %collective-permute-start.16 = (bf16[72,1664]{1,0:T(8,128)(2,1)S(1)}, bf16[72,1664]{1,0:T(8,128)(2,1)S(1)}, u32[]{:S(2)}, u32[]{:S(2)}) collective-permute-start(bf16[72,1664]{1,0:T(8,128)(2,1)S(1)} %get-tuple-element.97), channel_id=1, source_target_pairs={{0,4},{2,6},{4,0},{6,2},{8,12},{10,14},{12,8},{14,10},{1,5},{3,7},... | collective-permute-start | bytes 718856 | tf_op jit(solution)/shard_map/ppermute | solution.py:275
  10.2 11.8 %collective-permute-start.17 = (bf16[72,1664]{1,0:T(8,128)(2,1)S(1)}, bf16[72,1664]{1,0:T(8,128)(2,1)S(1)}, u32[]{:S(2)}, u32[]{:S(2)}) collective-permute-start(bf16[72,1664]{1,0:T(8,128)(2,1)S(1)} %get-tuple-element.98), channel_id=1, source_target_pairs={{0,6},{2,4},{4,2},{6,0},{8,14},{10,12},{12,10},{14,8},{1,7},{3,5},... | collective-permute-start | bytes 718856 | tf_op jit(solution)/shard_map/ppermute | solution.py:275
  11.8 0.7 copy-start.2
  12.4 0.7 copy-start.24
  13.1 14.2 %collective-permute-start.19 = (bf16[72,1536]{1,0:T(8,128)(2,1)}, bf16[72,1536]{1,0:T(8,128)(2,1)}, u32[]{:S(2)}, u32[]{:S(2)}) collective-permute-start(bf16[72,1536]{1,0:T(8,128)(2,1)} %get-tuple-element.109), channel_id=1, source_target_pairs={{0,2},{2,0},{4,6},{6,4},{8,10},{10,8},{12,14},{14,12},{1,3},{3,1},... | collective-permute-start | bytes 663560 | tf_op jit(solution)/shard_map/ppermute | solution.py:275
  15.0 14.8 %collective-permute-start.20 = (bf16[72,1536]{1,0:T(8,128)(2,1)}, bf16[72,1536]{1,0:T(8,128)(2,1)}, u32[]{:S(2)}, u32[]{:S(2)}) collective-permute-start(bf16[72,1536]{1,0:T(8,128)(2,1)} %get-tuple-element.110), channel_id=1, source_target_pairs={{0,4},{2,6},{4,0},{6,2},{8,12},{10,14},{12,8},{14,10},{1,5},{3,7},... | collective-permute-start | bytes 663560 | tf_op jit(solution)/shard_map/ppermute | solution.py:275
  16.6 0.9 %copy-start.3 = (bf16[72,1536]{1,0:T(8,128)(2,1)S(1)}, bf16[72,1536]{1,0:T(8,128)(2,1)}, u32[]{:S(2)}) copy-start(bf16[72,1536]{1,0:T(8,128)(2,1)} %copy-done.2) | copy-start | bytes 663556
  16.6 7.5 %copy-start.33 = (bf16[72,1664]{1,0:T(8,128)(2,1)S(1)}, bf16[72,1664]{1,0:T(8,128)(2,1)}, u32[]{:S(2)}) copy-start(bf16[72,1664]{1,0:T(8,128)(2,1)} %copy-done.32) | copy-start | bytes 718852
  17.6 16.3 %collective-permute-start.21 = (bf16[72,1536]{1,0:T(8,128)(2,1)S(1)}, bf16[72,1536]{1,0:T(8,128)(2,1)S(1)}, u32[]{:S(2)}, u32[]{:S(2)}) collective-permute-start(bf16[72,1536]{1,0:T(8,128)(2,1)S(1)} %copy-done.3), channel_id=1, source_target_pairs={{0,6},{2,4},{4,2},{6,0},{8,14},{10,12},{12,10},{14,8},{1,7},{3,5},... | collective-permute-start | bytes 663560 | tf_op jit(solution)/shard_map/ppermute | solution.py:275
  17.9 26.5 %collective-permute-start.23 = (bf16[72,2048]{1,0:T(8,128)(2,1)S(1)}, bf16[72,2048]{1,0:T(8,128)(2,1)S(1)}, u32[]{:S(2)}, u32[]{:S(2)}) collective-permute-start(bf16[72,2048]{1,0:T(8,128)(2,1)S(1)} %get-tuple-element.121), channel_id=1, source_target_pairs={{0,2},{2,0},{4,6},{6,4},{8,10},{10,8},{12,14},{14,12},{1,3},{3,1},... | collective-permute-start | bytes 884744 | tf_op jit(solution)/shard_map/ppermute | solution.py:275
  22.1 23.2 %collective-permute-start.24 = (bf16[72,2048]{1,0:T(8,128)(2,1)S(1)}, bf16[72,2048]{1,0:T(8,128)(2,1)S(1)}, u32[]{:S(2)}, u32[]{:S(2)}) collective-permute-start(bf16[72,2048]{1,0:T(8,128)(2,1)S(1)} %get-tuple-element.122), channel_id=1, source_target_pairs={{0,4},{2,6},{4,0},{6,2},{8,12},{10,14},{12,8},{14,10},{1,5},{3,7},... | collective-permute-start | bytes 884744 | tf_op jit(solution)/shard_map/ppermute | solution.py:275
  24.1 9.7 %copy-start.25 = (bf16[72,1536]{1,0:T(8,128)(2,1)S(1)}, bf16[72,1536]{1,0:T(8,128)(2,1)}, u32[]{:S(2)}) copy-start(bf16[72,1536]{1,0:T(8,128)(2,1)} %copy-done.24) | copy-start | bytes 663556
  27.4 22.9 %collective-permute-start.25 = (bf16[72,2048]{1,0:T(8,128)(2,1)S(1)}, bf16[72,2048]{1,0:T(8,128)(2,1)S(1)}, u32[]{:S(2)}, u32[]{:S(2)}) collective-permute-start(bf16[72,2048]{1,0:T(8,128)(2,1)S(1)} %get-tuple-element.123), channel_id=1, source_target_pairs={{0,6},{2,4},{4,2},{6,0},{8,14},{10,12},{12,10},{14,8},{1,7},{3,5},... | collective-permute-start | bytes 884744 | tf_op jit(solution)/shard_map/ppermute | solution.py:275
  29.9 25.2 %collective-permute-start.18 = (s16[64,1664]{1,0:T(8,128)(2,1)}, s16[64,1664]{1,0:T(8,128)(2,1)S(1)}, u32[]{:S(2)}, u32[]{:S(2)}) collective-permute-start(s16[64,1664]{1,0:T(8,128)(2,1)} %get-tuple-element.99), channel_id=1, source_target_pairs={{0,8},{2,10},{4,12},{6,14},{8,0},{10,2},{12,4},{14,6},{1,9},{3,11}... | collective-permute-start | bytes 638984 | tf_op jit(solution)/shard_map/ppermute | solution.py:336
  33.9 0.9 %copy-start.28 = (bf16[2,64,288]{2,1,0:T(8,128)(2,1)S(1)}, bf16[2,64,288]{2,1,0:T(8,128)(2,1)}, u32[]{:S(2)}) copy-start(bf16[2,64,288]{2,1,0:T(8,128)(2,1)} %get-tuple-element.103.refs_4_.refs_6_) | copy-start | bytes 221188
  34.8 0.9 %copy-start.38 = (bf16[288,128]{1,0:T(8,128)(2,1)S(1)}, bf16[288,128]{1,0:T(8,128)(2,1)}, u32[]{:S(2)}) copy-start(bf16[288,128]{1,0:T(8,128)(2,1)} %get-tuple-element.112.refs_4_) | copy-start | bytes 221188
  35.6 0.9 %copy-start.39 = (bf16[288,128]{1,0:T(8,128)(2,1)S(1)}, bf16[288,128]{1,0:T(8,128)(2,1)}, u32[]{:S(2)}) copy-start(bf16[288,128]{1,0:T(8,128)(2,1)} %get-tuple-element.113.refs_5_) | copy-start | bytes 221188
  36.5 13.8 %copy-start.29 = (bf16[2,64,288]{2,1,0:T(8,128)(2,1)S(1)}, bf16[2,64,288]{2,1,0:T(8,128)(2,1)}, u32[]{:S(2)}) copy-start(bf16[2,64,288]{2,1,0:T(8,128)(2,1)} %get-tuple-element.103.refs_4_.refs_6_) | copy-start | bytes 221188
  36.5 13.8 %copy-start.40 = (bf16[288,128]{1,0:T(8,128)(2,1)S(1)}, bf16[288,128]{1,0:T(8,128)(2,1)}, u32[]{:S(2)}) copy-start(bf16[288,128]{1,0:T(8,128)(2,1)} %get-tuple-element.113.refs_5_) | copy-start | bytes 221188
  40.1 16.6 %collective-permute-start.22 = (s16[64,1664]{1,0:T(8,128)(2,1)}, s16[64,1664]{1,0:T(8,128)(2,1)S(1)}, u32[]{:S(2)}, u32[]{:S(2)}) collective-permute-start(s16[64,1664]{1,0:T(8,128)(2,1)} %get-tuple-element.114), channel_id=1, source_target_pairs={{0,8},{2,10},{4,12},{6,14},{8,0},{10,2},{12,4},{14,6},{1,9},{3,11}... | collective-permute-start | bytes 638984 | tf_op jit(solution)/shard_map/ppermute | solution.py:336
  50.3 4.8 %copy-start.14 = (bf16[288,1536]{1,0:T(8,128)(2,1)S(1)}, bf16[288,1536]{1,0:T(8,128)(2,1)}, u32[]{:S(2)}) copy-start(bf16[288,1536]{1,0:T(8,128)(2,1)} %get-tuple-element.101.refs_2_) | copy-start | bytes 2654212
  50.3 4.8 %copy-start.15 = (bf16[288,1536]{1,0:T(8,128)(2,1)S(1)}, bf16[288,1536]{1,0:T(8,128)(2,1)}, u32[]{:S(2)}) copy-start(bf16[288,1536]{1,0:T(8,128)(2,1)} %get-tuple-element.102.refs_3_) | copy-start | bytes 2654212
  50.3 4.8 %copy-start.21 = (f32[64,1536]{1,0:T(8,128)S(1)}, f32[64,1536]{1,0:T(8,128)}, u32[]{:S(2)}) copy-start(f32[64,1536]{1,0:T(8,128)} %get-tuple-element.100.refs_1_) | copy-start | bytes 1179652
  53.5 14.9 %collective-permute-start.26 = (s16[64,2176]{1,0:T(8,128)(2,1)}, s16[64,2176]{1,0:T(8,128)(2,1)S(1)}, u32[]{:S(2)}, u32[]{:S(2)}) collective-permute-start(s16[64,2176]{1,0:T(8,128)(2,1)} %get-tuple-element.124), channel_id=1, source_target_pairs={{0,8},{2,10},{4,12},{6,14},{8,0},{10,2},{12,4},{14,6},{1,9},{3,11}... | collective-permute-start | bytes 835592 | tf_op jit(solution)/shard_map/ppermute | solution.py:336
  55.1 1.6 %copy-start.12 = (bf16[288,1536]{1,0:T(8,128)(2,1)S(1)}, bf16[288,1536]{1,0:T(8,128)(2,1)}, u32[]{:S(2)}) copy-start(bf16[288,1536]{1,0:T(8,128)(2,1)} %get-tuple-element.116.refs_2_) | copy-start | bytes 2654212
  55.1 1.6 %copy-start.13 = (bf16[288,1536]{1,0:T(8,128)(2,1)S(1)}, bf16[288,1536]{1,0:T(8,128)(2,1)}, u32[]{:S(2)}) copy-start(bf16[288,1536]{1,0:T(8,128)(2,1)} %get-tuple-element.117.refs_3_) | copy-start | bytes 2654212
  55.1 1.6 %copy-start.20 = (f32[64,1536]{1,0:T(8,128)S(1)}, f32[64,1536]{1,0:T(8,128)}, u32[]{:S(2)}) copy-start(f32[64,1536]{1,0:T(8,128)} %get-tuple-element.115.refs_1_) | copy-start | bytes 1179652
  56.7 11.7 %copy-start.10 = (bf16[288,2048]{1,0:T(8,128)(2,1)S(1)}, bf16[288,2048]{1,0:T(8,128)(2,1)}, u32[]{:S(2)}) copy-start(bf16[288,2048]{1,0:T(8,128)(2,1)} %get-tuple-element.126.refs_2_) | copy-start | bytes 3538948
  56.7 11.7 %copy-start.11 = (bf16[288,2048]{1,0:T(8,128)(2,1)S(1)}, bf16[288,2048]{1,0:T(8,128)(2,1)}, u32[]{:S(2)}) copy-start(bf16[288,2048]{1,0:T(8,128)(2,1)} %get-tuple-element.127.refs_3_) | copy-start | bytes 3538948
  56.7 11.7 %copy-start.17 = (f32[64,2048]{1,0:T(8,128)S(1)}, f32[64,2048]{1,0:T(8,128)}, u32[]{:S(2)}) copy-start(f32[64,2048]{1,0:T(8,128)} %get-tuple-element.125.refs_1_) | copy-start | bytes 1572868
  69.4 4.5 %collective-permute-start.29 = (f32[8,128]{1,0:T(8,128)S(1)}, f32[8,128]{1,0:T(8,128)S(1)}, u32[]{:S(2)}, u32[]{:S(2)}) collective-permute-start(f32[8,128]{1,0:T(8,128)S(1)} %get-tuple-element.130.refs_0_), channel_id=1, source_target_pairs={{6,0},{4,2},{2,4},{0,6},{14,8},{12,10},{10,12},{8,14},{7,1},{5,3},... | collective-permute-start | bytes 12296 | tf_op jit(solution)/shard_map/ppermute | solution.py:356
  69.4 4.5 %collective-permute-start.28 = (f32[8,128]{1,0:T(8,128)S(1)}, f32[8,128]{1,0:T(8,128)S(1)}, u32[]{:S(2)}, u32[]{:S(2)}) collective-permute-start(f32[8,128]{1,0:T(8,128)S(1)} %get-tuple-element.130.refs_0_), channel_id=1, source_target_pairs={{4,0},{6,2},{0,4},{2,6},{12,8},{14,10},{8,12},{10,14},{5,1},{7,3},... | collective-permute-start | bytes 12296 | tf_op jit(solution)/shard_map/ppermute | solution.py:356
  71.9 3.6 %collective-permute-start.27 = (f32[8,128]{1,0:T(8,128)S(1)}, f32[8,128]{1,0:T(8,128)S(1)}, u32[]{:S(2)}, u32[]{:S(2)}) collective-permute-start(f32[8,128]{1,0:T(8,128)S(1)} %get-tuple-element.130.refs_0_), channel_id=1, source_target_pairs={{2,0},{0,2},{6,4},{4,6},{10,8},{8,10},{14,12},{12,14},{3,1},{1,3},... | collective-permute-start | bytes 12296 | tf_op jit(solution)/shard_map/ppermute | solution.py:356
  73.3 2.5 %copy-start.42 = (bf16[224,2,2560]{2,1,0:T(2,128)(2,1)S(1)}, bf16[224,2,2560]{2,1,0:T(2,128)(2,1)}, u32[]{:S(2)}) copy-start(bf16[224,2,2560]{2,1,0:T(2,128)(2,1)} %x_ref.1) | copy-start | bytes 6881284
  73.3 2.5 %copy-start.45 = (s32[224,1]{0,1:T(1,128)S(1)}, s32[224,1]{0,1:T(1,128)}, u32[]{:S(2)}) copy-start(s32[224,1]{0,1:T(1,128)} %param.7) | copy-start | bytes 2692
  73.3 2.5 %copy-start.46 = (s32[224]{0:T(256)S(1)}, s32[224]{0:T(256)}, u32[]{:S(2)}) copy-start(s32[224]{0:T(256)} %param.8) | copy-start | bytes 2692
  73.3 2.5 %copy-start.47 = (s32[224]{0:T(256)S(1)}, s32[224]{0:T(256)}, u32[]{:S(2)}) copy-start(s32[224]{0:T(256)} %param.9) | copy-start | bytes 2692
  76.0 1.8 %copy-start.44 = (bf16[32,2,2560]{2,1,0:T(2,128)(2,1)}, bf16[32,2,2560]{2,1,0:T(2,128)(2,1)S(1)}, u32[]{:S(2)}) copy-start(bf16[32,2,2560]{2,1,0:T(2,128)(2,1)S(1)} %get-tuple-element.93) | copy-start | bytes 983044
  76.1 1.2 %collective-permute-start.30 = (f32[1,224]{1,0:T(1,128)S(1)}, f32[1,224]{1,0:T(1,128)S(1)}, u32[]{:S(2)}, u32[]{:S(2)}) collective-permute-start(f32[1,224]{1,0:T(1,128)S(1)} %get-tuple-element.132), channel_id=1, source_target_pairs={{0,1},{1,0},{2,3},{3,2},{4,5},{5,4},{6,7},{7,6},{8,9},{9,8},{10,11... | collective-permute-start | bytes 2696 | tf_op jit(solution)/shard_map/ppermute | solution.py:389

commit v3 on v2

--- a/solution.py
+++ b/solution.py
@@ -14,10 +14,9 @@
 CAP = 2
 LANES = 128
 BLOCK = 256
-SHARES = (0.3, 0.3, 0.4)
-PIN = 1
-GATE = 0
-HOLD = False
+SHARES = (0.3, 0.4, 0.3)
+PIN = (0, 1, 2, 3)
+KEEP = (0,)
 COST = 5
 FLOWS = (3, 1, 2)
 ROWS = 8
@@ -58,12 +57,9 @@
 
 
 def pack_first(
-    parts, cap, grid, width, x_ref, label_ref, angle_ref, count_ref, z_ref, column_ref, *refs
+    parts, cap, grid, lanes, width, x_ref, label_ref, angle_ref, count_ref, z_ref, column_ref, *out_refs
 ):
-    out_refs, (held_ref, semaphore) = refs[:-2], refs[-2:]
     n_dom, n_cls, pair = grid
-    copy = pltpu.make_async_copy(x_ref.at[:, :, pl.ds(0, width)], held_ref, semaphore)
-    copy.start()
     slot_ref = out_refs[parts]
     people = label_ref.shape[1]
     owned = CLASSES // (n_dom * n_cls)
@@ -96,8 +92,7 @@
     details = jnp.where(rows == 3, count_ref[...].astype(f32), details)
     details = details.astype(bf16)
     lane = lax.broadcasted_iota(i32, (cap, LANES), 1)
-    copy.wait()
-    real, imag = held_ref[:, 0, :], held_ref[:, 1, :]
+    real, imag = pick_lanes(x_ref, lanes, 0, width)
     for part in range(parts):
         place = place_of(slot - part * cap, cap)
         out_refs[part][:, :width] = matmul(place, real).astype(bf16)
@@ -228,12 +223,12 @@
     out_ref[...] = total[0:1] * (1.0 / math.sqrt(2.0 * NK * NQ))
 
 
-def call(kernel, outs, *args, work=1, scalars=0, pin=False, far=0, scratch=()):
+def call(kernel, outs, *args, work=1, scalars=0, pin=()):
     shapes = [
-        (pltpu.HBM if pin and math.prod(shape) > 1 << 15 else jax.ShapeDtypeStruct)(shape, dtype) for shape, dtype in outs
+        (pltpu.HBM if number in pin else jax.ShapeDtypeStruct)(shape, dtype)
+        for number, (shape, dtype) in enumerate(outs)
     ]
-    specs = [pl.BlockSpec(memory_space=pl.ANY)] * far
-    specs += [pl.BlockSpec(memory_space=pltpu.VMEM)] * (len(args) - scalars - far)
+    specs = [pl.BlockSpec(memory_space=pltpu.VMEM)] * (len(args) - scalars)
     specs += [pl.BlockSpec(memory_space=pltpu.SMEM)] * scalars
     places = [pl.BlockSpec(memory_space=pltpu.VMEM)] * len(outs)
     cost = pl.CostEstimate(flops=int(work * COST * 10**9), bytes_accessed=0, transcendentals=0) if COST else None
@@ -242,7 +237,6 @@
         in_specs=specs,
         out_specs=places,
         out_shape=shapes,
-        scratch_shapes=scratch,
         cost_estimate=cost,
         compiler_params=PARAMS,
     )(*args)
@@ -278,65 +272,61 @@
     lanes = -(-3 * nfreq // LANES) * LANES
     starts = [sum(sizes[:i]) for i in range(len(sizes))]
     core = lax.axis_index("coef").reshape(1, 1).astype(i32)
-    arrived = []
-    rest = None
+    arrived, codes, kept, tables = [], [], [], []
+    rest = particles.reshape(people, 2 * width)
+    slot = None
+
+    def turn(number):
+        start, freqs = starts[number], sizes[number]
+        wide = 2 * freqs * NQ
+        kernel = functools.partial(align, parts, cap, subs, nfreq, number == 0, freqs, start)
+        outs = [((subs, wide + LANES), jnp.int16), ((subs, wide), f32), ((rows, wide), bf16), ((rows, wide), bf16)]
+        if number == 0:
+            outs += [((rows, lanes), bf16)] * 2 + [((2, subs, rows), bf16), ((subs, LANES), f32)]
+            code, *held = call(kernel, outs, *arrived[0], core, scalars=1, work=4, pin=(*PIN, 6))
+            tables.extend(held[3:])
+        else:
+            code, *held = call(kernel, outs, *arrived[number], *tables[:3], work=3, pin=PIN)
+        codes.append(code)
+        kept.append(held[:3])
+
     for number, (start, freqs) in enumerate(zip(starts, sizes)):
         if number == 0:
             size = freqs * NQ
             *packed, slot = call(
-                functools.partial(pack_first, parts, cap, (n_dom, n_cls, pair), size),
+                functools.partial(pack_first, parts, cap, (n_dom, n_cls, pair), width, size),
                 [((cap, 2 * size + LANES), bf16)] * parts + [((8, people), i32)],
-                particles,
+                rest,
                 label,
                 angles[None],
                 counts[None],
                 lax.axis_index("dom").reshape(1, 1).astype(i32),
                 lax.axis_index("cls").reshape(1, 1).astype(i32),
                 scalars=2,
-                far=1,
                 work=3,
-                scratch=[pltpu.VMEM((people, 2, size), bf16), pltpu.SemaphoreType.DMA],
-                pin=PIN >= 2,
+                pin=KEEP,
             )
         else:
-            if number == 1:
-                rest = particles
-                if HOLD:
-                    rest, slot = lax.optimization_barrier((particles, slot))
-                rest = rest.reshape(people, 2 * width)
-            if GATE:
-                slot, arrived[-1][GATE] = lax.optimization_barrier((slot, arrived[-1][GATE]))
+            if number >= 2:
+                slot, codes[-1] = lax.optimization_barrier((slot, codes[-1]))
             packed = call(
                 functools.partial(pack_next, parts, cap, width, start * NQ, freqs * NQ),
                 [((cap, 2 * freqs * NQ), bf16)] * parts,
                 slot,
                 rest,
-                pin=PIN >= 2,
+                pin=KEEP,
             )
         arrived.append(deliver(packed))
-    aligned = []
-    for number, (start, freqs) in enumerate(zip(starts, sizes)):
-        wide = 2 * freqs * NQ
-        kernel = functools.partial(align, parts, cap, subs, nfreq, number == 0, freqs, start)
-        outs = [
-            ((subs, wide + LANES), jnp.int16),
-            ((subs, wide), f32),
-            ((rows, wide), bf16),
-            ((rows, wide), bf16),
-        ]
-        if number == 0:
-            more = [((rows, lanes), bf16)] * 2 + [((2, subs, rows), bf16), ((subs, LANES), f32)]
-            code, sums, high, mid, cosines, sines, hot, info = call(
-                kernel, outs + more, *arrived[0], core, scalars=1, work=4, pin=PIN >= 1
-            )
-        else:
-            code, sums, high, mid = call(
-                kernel, outs, *arrived[number], cosines, sines, hot, work=3, pin=PIN >= 1
-            )
-        codes = [lax.ppermute(code, axes, across(turn)) for turn in range(1, groups)]
-        aligned.append((codes, sums, high, mid))
+        if number >= 1:
+            turn(number - 1)
+    turn(len(sizes) - 1)
+    aligned = [
+        ([lax.ppermute(code, axes, across(step)) for step in range(1, groups)], *rows_of)
+        for code, rows_of in zip(codes, kept)
+    ]
     means = []
     gain = None
+    hot, info = tables[2:]
     for number, (codes, sums, high, mid) in enumerate(aligned):
         first, last = number == 0, number == len(sizes) - 1
         kernel = functools.partial(score, parts, cap, groups - 1, first, last)

time: 78.2 us -> 75 us (0.959)
  waiting for transfers between devices: 21.9 us -> 26.5 us
  local copies, waits for them, and re-layouts: 7.66 us -> 3.85 us
  Pallas kernels: 19 us -> 16.3 us
  starting transfers between devices: 26.6 us -> 25.6 us
    ppermute x9, waiting for transfers between devices: 9.81 us -> 13.3 us  [deliver(): taken[part] = lax.ppermute(packed[part], axes, forward(part))]
    pallas_call x10, Pallas kernels: 19 us -> 16.3 us  [call(): pl.pallas_call(kernel, in_specs=specs, out_specs=places, out_shape=shapes...]
    unnamed x53 -> x37, local copies, waits for them, and re-layouts: 5.31 us -> 3.01 us
    ppermute x3, starting transfers between devices: 8.54 us -> 6.53 us  [exchange(): lax.ppermute(code, axes, across(step))]
    ppermute x3, waiting for transfers between devices: 2.2 us -> 3.22 us  [exchange(): lax.ppermute(gain, axes, [(b, a) for a, b in forward(part)])]
    reshape x3, local copies, waits for them, and re-layouts: 1.03 us -> 0.14 us  [exchange(): lax.dynamic_slice_in_dim(mean, square * owned, owned).reshape(owned, 2, -1)]
    ppermute x9, starting transfers between devices: 14.5 us -> 15.3 us  [deliver(): taken[part] = lax.ppermute(packed[part], axes, forward(part))]
  transfers between devices with their start and end apart: 16 -> 16, of which waited for: 9 -> 11; matrix products, arithmetic and copies ran while one was open for 4% -> 2% of each run, Pallas kernels for 17% -> 18%
where the time goes in v3:
time: 75 us; the launch traced here: 74.8 us
  waiting for transfers between devices  26.5 us (35%)
  starting transfers between devices  25.6 us (34%)
  Pallas kernels  16.3 us (22%)
  local copies, waits for them, and re-layouts  3.85 us (5%)
  between operations  1.57 us (2%)
  other arithmetic  0.85 us (1%)
    pallas_call x10, Pallas kernels, call(): pl.pallas_call(kernel, in_specs=specs, out_specs=places, out_shape=shapes...  16.3 us
    ppermute x9, starting transfers between devices, deliver(): taken[part] = lax.ppermute(packed[part], axes, forward(part))  15.3 us
    ppermute x9, waiting for transfers between devices, deliver(): taken[part] = lax.ppermute(packed[part], axes, forward(part))  13.3 us
    ppermute x3, waiting for transfers between devices, exchange(): lax.ppermute(code, axes, across(step))  8.89 us
    ppermute x3, starting transfers between devices, exchange(): lax.ppermute(code, axes, across(step))  6.53 us
    ppermute x3, starting transfers between devices, exchange(): lax.ppermute(gain, axes, [(b, a) for a, b in forward(part)])  3.69 us
    ppermute x3, waiting for transfers between devices, exchange(): lax.ppermute(gain, axes, [(b, a) for a, b in forward(part)])  3.22 us
    unnamed x37, local copies, waits for them, and re-layouts  3.01 us
  transfers between devices with their start and end apart: 16, of which 11 were waited for; matrix products, arithmetic and copies ran while one was open for 2% of the time, Pallas kernels for 18%

profile of v3, /device:TPU:0, one launch (start us, length us, event | category | flops | bytes accessed | tf_op | source)
XLA Modules:
  0.0 74.8 jit_solution(11375852802230860331)
XLA Ops:
  0.7 2.0 %copy.7 = bf16[28,8,2,2560]{3,1,2,0:T(8,128)(2,1)S(1)} copy(bf16[28,8,2,2560]{3,2,1,0:T(2,128)(2,1)} %bitcast.23) | data formatting | bytes 4587520
  2.7 1.4 %shard_map.59 = (bf16[72,1664]{1,0:T(8,128)(2,1)}, bf16[72,1664]{1,0:T(8,128)(2,1)}, bf16[72,1664]{1,0:T(8,128)(2,1)}, bf16[72,1664]{1,0:T(8,128)(2,1)}, s32[8,224]{1,0:T(8,128)S(1)}) custom-call(bf16[224,5120]{1,0:T(8,128)(2,1)S(1)} %bitcast.17, s32[1,224]{1,0:T(1,128)S(1)} %bitcast.26, s32[1,224]{1,0:T(1,128)S(1)} %bitcast.28, s32[1,224]{1,0:T(1,128)S(1)} %bitcast.30, ...), custom_call_target="tpu_custom_call" | custom-call | flops 15000000512 | tf_op jit(solution)/shard_map/pallas_call | solution.py:235
  4.1 2.9 %collective-permute-start.15 = (bf16[72,1664]{1,0:T(8,128)(2,1)}, bf16[72,1664]{1,0:T(8,128)(2,1)}, u32[]{:S(2)}, u32[]{:S(2)}) collective-permute-start(bf16[72,1664]{1,0:T(8,128)(2,1)} %get-tuple-element.101), channel_id=1, source_target_pairs={{0,2},{2,0},{4,6},{6,4},{8,10},{10,8},{12,14},{14,12},{1,3},{3,1},... | collective-permute-start | bytes 718856 | tf_op jit(solution)/shard_map/ppermute | solution.py:269
  7.1 1.6 %collective-permute-start.16 = (bf16[72,1664]{1,0:T(8,128)(2,1)}, bf16[72,1664]{1,0:T(8,128)(2,1)}, u32[]{:S(2)}, u32[]{:S(2)}) collective-permute-start(bf16[72,1664]{1,0:T(8,128)(2,1)} %get-tuple-element.102), channel_id=1, source_target_pairs={{0,4},{2,6},{4,0},{6,2},{8,12},{10,14},{12,8},{14,10},{1,5},{3,7},... | collective-permute-start | bytes 718856 | tf_op jit(solution)/shard_map/ppermute | solution.py:269
  8.7 0.0 collective-permute-start.17
  8.7 1.2 %shard_map.62 = (bf16[72,2048]{1,0:T(8,128)(2,1)}, bf16[72,2048]{1,0:T(8,128)(2,1)}, bf16[72,2048]{1,0:T(8,128)(2,1)S(1)}, bf16[72,2048]{1,0:T(8,128)(2,1)S(1)}) custom-call(s32[8,224]{1,0:T(8,128)S(1)} %get-tuple-element.125.slot_ref, bf16[224,5120]{1,0:T(8,128)(2,1)S(1)} %bitcast.18), custom_call_target="tpu_custom_call" | custom-call | flops 5000000000 | tf_op jit(solution)/shard_map/pallas_call | solution.py:235
  9.9 1.9 %collective-permute-start.19 = (bf16[72,2048]{1,0:T(8,128)(2,1)}, bf16[72,2048]{1,0:T(8,128)(2,1)S(1)}, u32[]{:S(2)}, u32[]{:S(2)}) collective-permute-start(bf16[72,2048]{1,0:T(8,128)(2,1)} %get-tuple-element.114), channel_id=1, source_target_pairs={{0,2},{2,0},{4,6},{6,4},{8,10},{10,8},{12,14},{14,12},{1,3},{3,1},... | collective-permute-start | bytes 884744 | tf_op jit(solution)/shard_map/ppermute | solution.py:269
  11.8 1.6 %collective-permute-start.20 = (bf16[72,2048]{1,0:T(8,128)(2,1)S(1)}, bf16[72,2048]{1,0:T(8,128)(2,1)S(1)}, u32[]{:S(2)}, u32[]{:S(2)}) collective-permute-start(bf16[72,2048]{1,0:T(8,128)(2,1)S(1)} %get-tuple-element.115), channel_id=1, source_target_pairs={{0,4},{2,6},{4,0},{6,2},{8,12},{10,14},{12,8},{14,10},{1,5},{3,7},... | collective-permute-start | bytes 884744 | tf_op jit(solution)/shard_map/ppermute | solution.py:269
  13.4 1.4 %collective-permute-done.15.refs_1_ = bf16[72,1664]{1,0:T(8,128)(2,1)} collective-permute-done((bf16[72,1664]{1,0:T(8,128)(2,1)}, bf16[72,1664]{1,0:T(8,128)(2,1)}, u32[]{:S(2)}, u32[]{:S(2)}) %collective-permute-start.15) | collective-permute-done | bytes 239648 | tf_op jit(solution)/shard_map/ppermute | solution.py:269
  14.7 3.8 %collective-permute-start.21 = (bf16[72,2048]{1,0:T(8,128)(2,1)S(1)}, bf16[72,2048]{1,0:T(8,128)(2,1)S(1)}, u32[]{:S(2)}, u32[]{:S(2)}) collective-permute-start(bf16[72,2048]{1,0:T(8,128)(2,1)S(1)} %get-tuple-element.116), channel_id=1, source_target_pairs={{0,6},{2,4},{4,2},{6,0},{8,14},{10,12},{12,10},{14,8},{1,7},{3,5},... | collective-permute-start | bytes 884744 | tf_op jit(solution)/shard_map/ppermute | solution.py:269
  18.5 0.0 collective-permute-done.16.refs_2_
  18.5 2.3 %collective-permute-done.17.refs_3_ = bf16[72,1664]{1,0:T(8,128)(2,1)} collective-permute-done((bf16[72,1664]{1,0:T(8,128)(2,1)}, bf16[72,1664]{1,0:T(8,128)(2,1)}, u32[]{:S(2)}, u32[]{:S(2)}) %collective-permute-start.17) | collective-permute-done | bytes 239648 | tf_op jit(solution)/shard_map/ppermute | solution.py:269
  20.8 0.9 %copy-done.27 = bf16[72,1664]{1,0:T(8,128)(2,1)S(1)} copy-done((bf16[72,1664]{1,0:T(8,128)(2,1)S(1)}, bf16[72,1664]{1,0:T(8,128)(2,1)}, u32[]{:S(2)}) %copy-start.27) | copy-done | bytes 239640
  21.8 4.3 %shard_map.60 = (s16[64,1664]{1,0:T(8,128)(2,1)}, f32[64,1536]{1,0:T(8,128)}, bf16[288,1536]{1,0:T(8,128)(2,1)}, bf16[288,1536]{1,0:T(8,128)(2,1)}, bf16[288,128...) custom-call(bf16[72,1664]{1,0:T(8,128)(2,1)S(1)} %copy-done.27, ...), custom_call_target="tpu_custom_call" | custom-call | flops 20000000000 | tf_op jit(solution)/shard_map/pallas_call | solution.py:235
  26.1 3.1 %collective-permute-start.18 = (s16[64,1664]{1,0:T(8,128)(2,1)}, s16[64,1664]{1,0:T(8,128)(2,1)S(1)}, u32[]{:S(2)}, u32[]{:S(2)}) collective-permute-start(s16[64,1664]{1,0:T(8,128)(2,1)} %get-tuple-element.105), channel_id=1, source_target_pairs={{0,8},{2,10},{4,12},{6,14},{8,0},{10,2},{12,4},{14,6},{1,9},{3,11}... | collective-permute-start | bytes 638984 | tf_op jit(solution)/shard_map/ppermute | solution.py:324
  29.3 1.0 %shard_map.65 = (bf16[72,1536]{1,0:T(8,128)(2,1)}, bf16[72,1536]{1,0:T(8,128)(2,1)S(1)}, bf16[72,1536]{1,0:T(8,128)(2,1)S(1)}, bf16[72,1536]{1,0:T(8,128)(2,1)S(1)}) custom-call(s32[8,224]{1,0:T(8,128)S(1)} %get-tuple-element.125.slot_ref, bf16[224,5120]{1,0:T(8,128)(2,1)S(1)} %bitcast.19), custom_call_target="tpu_custom_call" | custom-call | flops 5000000000 | tf_op jit(solution)/shard_map/pallas_call | solution.py:235
  30.2 1.5 %collective-permute-start.23 = (bf16[72,1536]{1,0:T(8,128)(2,1)S(1)}, bf16[72,1536]{1,0:T(8,128)(2,1)S(1)}, u32[]{:S(2)}, u32[]{:S(2)}) collective-permute-start(bf16[72,1536]{1,0:T(8,128)(2,1)S(1)} %get-tuple-element.127), channel_id=1, source_target_pairs={{0,2},{2,0},{4,6},{6,4},{8,10},{10,8},{12,14},{14,12},{1,3},{3,1},... | collective-permute-start | bytes 663560 | tf_op jit(solution)/shard_map/ppermute | solution.py:269
  31.7 0.0 collective-permute-done.19.refs_1_
  31.7 1.6 %collective-permute-start.24 = (bf16[72,1536]{1,0:T(8,128)(2,1)S(1)}, bf16[72,1536]{1,0:T(8,128)(2,1)S(1)}, u32[]{:S(2)}, u32[]{:S(2)}) collective-permute-start(bf16[72,1536]{1,0:T(8,128)(2,1)S(1)} %get-tuple-element.128), channel_id=1, source_target_pairs={{0,4},{2,6},{4,0},{6,2},{8,12},{10,14},{12,8},{14,10},{1,5},{3,7},... | collective-permute-start | bytes 663560 | tf_op jit(solution)/shard_map/ppermute | solution.py:269
  33.3 0.0 collective-permute-done.20.refs_2_
  33.3 0.4 collective-permute-start.25
  33.7 4.2 %collective-permute-done.21.refs_3_ = bf16[72,2048]{1,0:T(8,128)(2,1)S(1)} collective-permute-done((bf16[72,2048]{1,0:T(8,128)(2,1)S(1)}, bf16[72,2048]{1,0:T(8,128)(2,1)S(1)}, u32[]{:S(2)}, u32[]{:S(2)}) %collective-permute-start.21) | collective-permute-done | bytes 294944 | tf_op jit(solution)/shard_map/ppermute | solution.py:269
  38.0 3.1 %shard_map.63 = (s16[64,2176]{1,0:T(8,128)(2,1)}, f32[64,2048]{1,0:T(8,128)}, bf16[288,2048]{1,0:T(8,128)(2,1)}, bf16[288,2048]{1,0:T(8,128)(2,1)}) custom-call(bf16[72,2048]{1,0:T(8,128)(2,1)S(1)} %copy-done.21, bf16[72,2048]{1,0:T(8,128)(2,1)S(1)} %collective-permute-done.19.refs_1_, bf16[72,2048]{1,0:T(8,128)(2,1)S(1)} %collective-permute-done.20.refs_2_, ...), custom_call_target="tpu_custom_call" | custom-call | flops 15000000512 | tf_op jit(solution)/shard_map/pallas_call | solution.py:235
  41.1 2.2 %collective-permute-start.22 = (s16[64,2176]{1,0:T(8,128)(2,1)}, s16[64,2176]{1,0:T(8,128)(2,1)S(1)}, u32[]{:S(2)}, u32[]{:S(2)}) collective-permute-start(s16[64,2176]{1,0:T(8,128)(2,1)} %get-tuple-element.119), channel_id=1, source_target_pairs={{0,8},{2,10},{4,12},{6,14},{8,0},{10,2},{12,4},{14,6},{1,9},{3,11}... | collective-permute-start | bytes 835592 | tf_op jit(solution)/shard_map/ppermute | solution.py:324
  43.3 0.0 collective-permute-done.18.refs_0_
  43.3 0.7 shard_map.61
  44.1 0.7 slice.3
  45.4 2.3 %collective-permute-done.24.refs_2_ = bf16[72,1536]{1,0:T(8,128)(2,1)S(1)} collective-permute-done((bf16[72,1536]{1,0:T(8,128)(2,1)S(1)}, bf16[72,1536]{1,0:T(8,128)(2,1)S(1)}, u32[]{:S(2)}, u32[]{:S(2)}) %collective-permute-start.24) | collective-permute-done | bytes 221216 | tf_op jit(solution)/shard_map/ppermute | solution.py:269
  47.7 3.1 %collective-permute-done.25.refs_3_ = bf16[72,1536]{1,0:T(8,128)(2,1)S(1)} collective-permute-done((bf16[72,1536]{1,0:T(8,128)(2,1)S(1)}, bf16[72,1536]{1,0:T(8,128)(2,1)S(1)}, u32[]{:S(2)}, u32[]{:S(2)}) %collective-permute-start.25) | collective-permute-done | bytes 221216 | tf_op jit(solution)/shard_map/ppermute | solution.py:269
  50.8 2.5 %shard_map.66 = (s16[64,1664]{1,0:T(8,128)(2,1)}, f32[64,1536]{1,0:T(8,128)}, bf16[288,1536]{1,0:T(8,128)(2,1)}, bf16[288,1536]{1,0:T(8,128)(2,1)}) custom-call(bf16[72,1536]{1,0:T(8,128)(2,1)S(1)} %copy-done.22, bf16[72,1536]{1,0:T(8,128)(2,1)S(1)} %collective-permute-done.23.refs_1_, bf16[72,1536]{1,0:T(8,128)(2,1)S(1)} %collective-permute-done.24.refs_2_, ...), custom_call_target="tpu_custom_call" | custom-call | flops 15000000512 | tf_op jit(solution)/shard_map/pallas_call | solution.py:235
  53.3 1.2 %collective-permute-start.26 = (s16[64,1664]{1,0:T(8,128)(2,1)}, s16[64,1664]{1,0:T(8,128)(2,1)S(1)}, u32[]{:S(2)}, u32[]{:S(2)}) collective-permute-start(s16[64,1664]{1,0:T(8,128)(2,1)} %get-tuple-element.130), channel_id=1, source_target_pairs={{0,8},{2,10},{4,12},{6,14},{8,0},{10,2},{12,4},{14,6},{1,9},{3,11}... | collective-permute-start | bytes 638984 | tf_op jit(solution)/shard_map/ppermute | solution.py:324
  54.5 0.3 collective-permute-done.22.refs_0_
  54.8 0.9 %shard_map.64 = (bf16[64,2048]{1,0:T(8,128)(2,1)S(1)}, f32[8,288]{1,0:T(8,128)S(1)}) custom-call(s16[64,2176]{1,0:T(8,128)(2,1)S(1)} %collective-permute-done.22.refs_0_, f32[64,2048]{1,0:T(8,128)S(1)} %copy-done.14, bf16[288,2048]{1,0:T(8,128)(2,1)S(1)} %copy-done.7, bf16[288,2048]{1,0:T(8,128)(2,1)S(1)} %copy-done.8, bf16[2,64,288]{2,1,0:T(8,128)(2,1)S(1)} %copy-done.24, ...), custom_call_target="tpu_custom_call" | custom-call | flops 5000000000 | tf_op jit(solution)/shard_map/pallas_call | solution.py:235
  55.8 0.1 reshape.62
  55.9 8.6 %collective-permute-done.26.refs_0_ = s16[64,1664]{1,0:T(8,128)(2,1)S(1)} collective-permute-done((s16[64,1664]{1,0:T(8,128)(2,1)}, s16[64,1664]{1,0:T(8,128)(2,1)S(1)}, u32[]{:S(2)}, u32[]{:S(2)}) %collective-permute-start.26) | collective-permute-done | bytes 213024 | tf_op jit(solution)/shard_map/ppermute | solution.py:324
  64.5 0.8 %shard_map.67 = (bf16[64,1536]{1,0:T(8,128)(2,1)S(1)}, f32[8,128]{1,0:T(8,128)S(1)}) custom-call(s16[64,1664]{1,0:T(8,128)(2,1)S(1)} %collective-permute-done.26.refs_0_, f32[64,1536]{1,0:T(8,128)S(1)} %copy-done.18, bf16[288,1536]{1,0:T(8,128)(2,1)S(1)} %copy-done.9, bf16[288,1536]{1,0:T(8,128)(2,1)S(1)} %copy-done.10, bf16[2,64,288]{2,1,0:T(8,128)(2,1)S(1)} %copy-done.25, ...), custom_call_target="tpu_custom_call" | custom-call | flops 5000000000 | tf_op jit(solution)/shard_map/pallas_call | solution.py:235
  65.4 1.1 %collective-permute-start.29 = (f32[8,128]{1,0:T(8,128)S(1)}, f32[8,128]{1,0:T(8,128)S(1)}, u32[]{:S(2)}, u32[]{:S(2)}) collective-permute-start(f32[8,128]{1,0:T(8,128)S(1)} %get-tuple-element.136.refs_0_), channel_id=1, source_target_pairs={{6,0},{4,2},{2,4},{0,6},{14,8},{12,10},{10,12},{8,14},{7,1},{5,3},... | collective-permute-start | bytes 12296 | tf_op jit(solution)/shard_map/ppermute | solution.py:346
  66.4 2.6 %collective-permute-start.28 = (f32[8,128]{1,0:T(8,128)S(1)}, f32[8,128]{1,0:T(8,128)S(1)}, u32[]{:S(2)}, u32[]{:S(2)}) collective-permute-start(f32[8,128]{1,0:T(8,128)S(1)} %get-tuple-element.136.refs_0_), channel_id=1, source_target_pairs={{4,0},{6,2},{0,4},{2,6},{12,8},{14,10},{8,12},{10,14},{5,1},{7,3},... | collective-permute-start | bytes 12296 | tf_op jit(solution)/shard_map/ppermute | solution.py:346
  69.1 0.3 pad_maximum_fusion.1
  69.4 0.4 collective-permute-done.29.refs_3_
  69.9 0.8 %collective-permute-done.28.refs_2_ = f32[8,128]{1,0:T(8,128)S(1)} collective-permute-done((f32[8,128]{1,0:T(8,128)S(1)}, f32[8,128]{1,0:T(8,128)S(1)}, u32[]{:S(2)}, u32[]{:S(2)}) %collective-permute-start.28) | collective-permute-done | bytes 4128 | tf_op jit(solution)/shard_map/ppermute | solution.py:346
  70.7 2.0 %collective-permute-done.27.refs_1_ = f32[8,128]{1,0:T(8,128)S(1)} collective-permute-done((f32[8,128]{1,0:T(8,128)S(1)}, f32[8,128]{1,0:T(8,128)S(1)}, u32[]{:S(2)}, u32[]{:S(2)}) %collective-permute-start.27) | collective-permute-done | bytes 4128 | tf_op jit(solution)/shard_map/ppermute | solution.py:346
  72.7 0.3 shard_map.68
  72.9 0.1 conditional.1
  73.0 0.0 copy-start.28
  73.1 0.1 collective-permute-start.30
  73.1 1.1 %collective-permute-done.30 = f32[1,224]{1,0:T(1,128)S(1)} collective-permute-done((f32[1,224]{1,0:T(1,128)S(1)}, f32[1,224]{1,0:T(1,128)S(1)}, u32[]{:S(2)}, u32[]{:S(2)}) %collective-permute-start.30) | collective-permute-done | bytes 928 | tf_op jit(solution)/shard_map/ppermute | solution.py:379
  74.3 0.6 add.16
  (40 shorter events, 0.2 us)
Async XLA Ops:
  0.6 2.0 %copy-start.29 = (s32[224,1]{0,1:T(1,128)S(1)}, s32[224,1]{0,1:T(1,128)}, u32[]{:S(2)}) copy-start(s32[224,1]{0,1:T(1,128)} %param.7) | copy-start | bytes 2692
  0.6 2.0 %copy-start.30 = (s32[224]{0:T(256)S(1)}, s32[224]{0:T(256)}, u32[]{:S(2)}) copy-start(s32[224]{0:T(256)} %param.8) | copy-start | bytes 2692
  0.7 2.0 %copy-start.31 = (s32[224]{0:T(256)S(1)}, s32[224]{0:T(256)}, u32[]{:S(2)}) copy-start(s32[224]{0:T(256)} %param.9) | copy-start | bytes 2692
  4.1 10.6 %collective-permute-start.15 = (bf16[72,1664]{1,0:T(8,128)(2,1)}, bf16[72,1664]{1,0:T(8,128)(2,1)}, u32[]{:S(2)}, u32[]{:S(2)}) collective-permute-start(bf16[72,1664]{1,0:T(8,128)(2,1)} %get-tuple-element.101), channel_id=1, source_target_pairs={{0,2},{2,0},{4,6},{6,4},{8,10},{10,8},{12,14},{14,12},{1,3},{3,1},... | collective-permute-start | bytes 718856 | tf_op jit(solution)/shard_map/ppermute | solution.py:269
  7.1 11.5 %collective-permute-start.16 = (bf16[72,1664]{1,0:T(8,128)(2,1)}, bf16[72,1664]{1,0:T(8,128)(2,1)}, u32[]{:S(2)}, u32[]{:S(2)}) collective-permute-start(bf16[72,1664]{1,0:T(8,128)(2,1)} %get-tuple-element.102), channel_id=1, source_target_pairs={{0,4},{2,6},{4,0},{6,2},{8,12},{10,14},{12,8},{14,10},{1,5},{3,7},... | collective-permute-start | bytes 718856 | tf_op jit(solution)/shard_map/ppermute | solution.py:269
  8.7 12.2 %collective-permute-start.17 = (bf16[72,1664]{1,0:T(8,128)(2,1)}, bf16[72,1664]{1,0:T(8,128)(2,1)}, u32[]{:S(2)}, u32[]{:S(2)}) collective-permute-start(bf16[72,1664]{1,0:T(8,128)(2,1)} %get-tuple-element.103), channel_id=1, source_target_pairs={{0,6},{2,4},{4,2},{6,0},{8,14},{10,12},{12,10},{14,8},{1,7},{3,5},... | collective-permute-start | bytes 718856 | tf_op jit(solution)/shard_map/ppermute | solution.py:269
  9.9 21.9 %collective-permute-start.19 = (bf16[72,2048]{1,0:T(8,128)(2,1)}, bf16[72,2048]{1,0:T(8,128)(2,1)S(1)}, u32[]{:S(2)}, u32[]{:S(2)}) collective-permute-start(bf16[72,2048]{1,0:T(8,128)(2,1)} %get-tuple-element.114), channel_id=1, source_target_pairs={{0,2},{2,0},{4,6},{6,4},{8,10},{10,8},{12,14},{14,12},{1,3},{3,1},... | collective-permute-start | bytes 884744 | tf_op jit(solution)/shard_map/ppermute | solution.py:269
  11.8 21.5 %collective-permute-start.20 = (bf16[72,2048]{1,0:T(8,128)(2,1)S(1)}, bf16[72,2048]{1,0:T(8,128)(2,1)S(1)}, u32[]{:S(2)}, u32[]{:S(2)}) collective-permute-start(bf16[72,2048]{1,0:T(8,128)(2,1)S(1)} %get-tuple-element.115), channel_id=1, source_target_pairs={{0,4},{2,6},{4,0},{6,2},{8,12},{10,14},{12,8},{14,10},{1,5},{3,7},... | collective-permute-start | bytes 884744 | tf_op jit(solution)/shard_map/ppermute | solution.py:269
  14.7 23.2 %collective-permute-start.21 = (bf16[72,2048]{1,0:T(8,128)(2,1)S(1)}, bf16[72,2048]{1,0:T(8,128)(2,1)S(1)}, u32[]{:S(2)}, u32[]{:S(2)}) collective-permute-start(bf16[72,2048]{1,0:T(8,128)(2,1)S(1)} %get-tuple-element.116), channel_id=1, source_target_pairs={{0,6},{2,4},{4,2},{6,0},{8,14},{10,12},{12,10},{14,8},{1,7},{3,5},... | collective-permute-start | bytes 884744 | tf_op jit(solution)/shard_map/ppermute | solution.py:269
  20.8 0.9 %copy-start.27 = (bf16[72,1664]{1,0:T(8,128)(2,1)S(1)}, bf16[72,1664]{1,0:T(8,128)(2,1)}, u32[]{:S(2)}) copy-start(bf16[72,1664]{1,0:T(8,128)(2,1)} %get-tuple-element.100.refs_0_) | copy-start | bytes 718852
  26.1 11.9 %copy-start.21 = (bf16[72,2048]{1,0:T(8,128)(2,1)S(1)}, bf16[72,2048]{1,0:T(8,128)(2,1)}, u32[]{:S(2)}) copy-start(bf16[72,2048]{1,0:T(8,128)(2,1)} %get-tuple-element.113.refs_0_) | copy-start | bytes 884740
  26.1 11.9 %copy-start.24 = (bf16[2,64,288]{2,1,0:T(8,128)(2,1)S(1)}, bf16[2,64,288]{2,1,0:T(8,128)(2,1)}, u32[]{:S(2)}) copy-start(bf16[2,64,288]{2,1,0:T(8,128)(2,1)} %get-tuple-element.109.refs_4_.refs_6_) | copy-start | bytes 221188
  26.1 17.2 %collective-permute-start.18 = (s16[64,1664]{1,0:T(8,128)(2,1)}, s16[64,1664]{1,0:T(8,128)(2,1)S(1)}, u32[]{:S(2)}, u32[]{:S(2)}) collective-permute-start(s16[64,1664]{1,0:T(8,128)(2,1)} %get-tuple-element.105), channel_id=1, source_target_pairs={{0,8},{2,10},{4,12},{6,14},{8,0},{10,2},{12,4},{14,6},{1,9},{3,11}... | collective-permute-start | bytes 638984 | tf_op jit(solution)/shard_map/ppermute | solution.py:324
  30.2 15.2 %collective-permute-start.23 = (bf16[72,1536]{1,0:T(8,128)(2,1)S(1)}, bf16[72,1536]{1,0:T(8,128)(2,1)S(1)}, u32[]{:S(2)}, u32[]{:S(2)}) collective-permute-start(bf16[72,1536]{1,0:T(8,128)(2,1)S(1)} %get-tuple-element.127), channel_id=1, source_target_pairs={{0,2},{2,0},{4,6},{6,4},{8,10},{10,8},{12,14},{14,12},{1,3},{3,1},... | collective-permute-start | bytes 663560 | tf_op jit(solution)/shard_map/ppermute | solution.py:269
  31.7 16.0 %collective-permute-start.24 = (bf16[72,1536]{1,0:T(8,128)(2,1)S(1)}, bf16[72,1536]{1,0:T(8,128)(2,1)S(1)}, u32[]{:S(2)}, u32[]{:S(2)}) collective-permute-start(bf16[72,1536]{1,0:T(8,128)(2,1)S(1)} %get-tuple-element.128), channel_id=1, source_target_pairs={{0,4},{2,6},{4,0},{6,2},{8,12},{10,14},{12,8},{14,10},{1,5},{3,7},... | collective-permute-start | bytes 663560 | tf_op jit(solution)/shard_map/ppermute | solution.py:269
  33.3 17.5 %collective-permute-start.25 = (bf16[72,1536]{1,0:T(8,128)(2,1)S(1)}, bf16[72,1536]{1,0:T(8,128)(2,1)S(1)}, u32[]{:S(2)}, u32[]{:S(2)}) collective-permute-start(bf16[72,1536]{1,0:T(8,128)(2,1)S(1)} %get-tuple-element.129), channel_id=1, source_target_pairs={{0,6},{2,4},{4,2},{6,0},{8,14},{10,12},{12,10},{14,8},{1,7},{3,5},... | collective-permute-start | bytes 663560 | tf_op jit(solution)/shard_map/ppermute | solution.py:269
  38.0 5.3 %copy-start.11 = (bf16[288,1536]{1,0:T(8,128)(2,1)S(1)}, bf16[288,1536]{1,0:T(8,128)(2,1)}, u32[]{:S(2)}) copy-start(bf16[288,1536]{1,0:T(8,128)(2,1)} %get-tuple-element.107.refs_2_) | copy-start | bytes 2654212
  38.0 5.3 %copy-start.12 = (bf16[288,1536]{1,0:T(8,128)(2,1)S(1)}, bf16[288,1536]{1,0:T(8,128)(2,1)}, u32[]{:S(2)}) copy-start(bf16[288,1536]{1,0:T(8,128)(2,1)} %get-tuple-element.108.refs_3_) | copy-start | bytes 2654212
  38.0 5.3 %copy-start.19 = (f32[64,1536]{1,0:T(8,128)S(1)}, f32[64,1536]{1,0:T(8,128)}, u32[]{:S(2)}) copy-start(f32[64,1536]{1,0:T(8,128)} %get-tuple-element.106.refs_1_) | copy-start | bytes 1179652
  41.1 13.7 %collective-permute-start.22 = (s16[64,2176]{1,0:T(8,128)(2,1)}, s16[64,2176]{1,0:T(8,128)(2,1)S(1)}, u32[]{:S(2)}, u32[]{:S(2)}) collective-permute-start(s16[64,2176]{1,0:T(8,128)(2,1)} %get-tuple-element.119), channel_id=1, source_target_pairs={{0,8},{2,10},{4,12},{6,14},{8,0},{10,2},{12,4},{14,6},{1,9},{3,11}... | collective-permute-start | bytes 835592 | tf_op jit(solution)/shard_map/ppermute | solution.py:324
  43.3 7.5 %copy-start.22 = (bf16[72,1536]{1,0:T(8,128)(2,1)S(1)}, bf16[72,1536]{1,0:T(8,128)(2,1)}, u32[]{:S(2)}) copy-start(bf16[72,1536]{1,0:T(8,128)(2,1)} %get-tuple-element.126.refs_0_) | copy-start | bytes 663556
  50.8 4.0 %copy-start.7 = (bf16[288,2048]{1,0:T(8,128)(2,1)S(1)}, bf16[288,2048]{1,0:T(8,128)(2,1)}, u32[]{:S(2)}) copy-start(bf16[288,2048]{1,0:T(8,128)(2,1)} %get-tuple-element.121.refs_2_) | copy-start | bytes 3538948
  50.8 4.0 %copy-start.8 = (bf16[288,2048]{1,0:T(8,128)(2,1)S(1)}, bf16[288,2048]{1,0:T(8,128)(2,1)}, u32[]{:S(2)}) copy-start(bf16[288,2048]{1,0:T(8,128)(2,1)} %get-tuple-element.122.refs_3_) | copy-start | bytes 3538948
  50.8 4.0 %copy-start.14 = (f32[64,2048]{1,0:T(8,128)S(1)}, f32[64,2048]{1,0:T(8,128)}, u32[]{:S(2)}) copy-start(f32[64,2048]{1,0:T(8,128)} %get-tuple-element.120.refs_1_) | copy-start | bytes 1572868
  53.3 11.2 %collective-permute-start.26 = (s16[64,1664]{1,0:T(8,128)(2,1)}, s16[64,1664]{1,0:T(8,128)(2,1)S(1)}, u32[]{:S(2)}, u32[]{:S(2)}) collective-permute-start(s16[64,1664]{1,0:T(8,128)(2,1)} %get-tuple-element.130), channel_id=1, source_target_pairs={{0,8},{2,10},{4,12},{6,14},{8,0},{10,2},{12,4},{14,6},{1,9},{3,11}... | collective-permute-start | bytes 638984 | tf_op jit(solution)/shard_map/ppermute | solution.py:324
  54.8 9.7 %copy-start.9 = (bf16[288,1536]{1,0:T(8,128)(2,1)S(1)}, bf16[288,1536]{1,0:T(8,128)(2,1)}, u32[]{:S(2)}) copy-start(bf16[288,1536]{1,0:T(8,128)(2,1)} %get-tuple-element.132.refs_2_) | copy-start | bytes 2654212
  54.8 9.7 %copy-start.10 = (bf16[288,1536]{1,0:T(8,128)(2,1)S(1)}, bf16[288,1536]{1,0:T(8,128)(2,1)}, u32[]{:S(2)}) copy-start(bf16[288,1536]{1,0:T(8,128)(2,1)} %get-tuple-element.133.refs_3_) | copy-start | bytes 2654212
  54.8 9.7 %copy-start.18 = (f32[64,1536]{1,0:T(8,128)S(1)}, f32[64,1536]{1,0:T(8,128)}, u32[]{:S(2)}) copy-start(f32[64,1536]{1,0:T(8,128)} %get-tuple-element.131.refs_1_) | copy-start | bytes 1179652
  54.8 9.7 %copy-start.25 = (bf16[2,64,288]{2,1,0:T(8,128)(2,1)S(1)}, bf16[2,64,288]{2,1,0:T(8,128)(2,1)}, u32[]{:S(2)}) copy-start(bf16[2,64,288]{2,1,0:T(8,128)(2,1)} %get-tuple-element.109.refs_4_.refs_6_) | copy-start | bytes 221188
  65.4 4.5 %collective-permute-start.29 = (f32[8,128]{1,0:T(8,128)S(1)}, f32[8,128]{1,0:T(8,128)S(1)}, u32[]{:S(2)}, u32[]{:S(2)}) collective-permute-start(f32[8,128]{1,0:T(8,128)S(1)} %get-tuple-element.136.refs_0_), channel_id=1, source_target_pairs={{6,0},{4,2},{2,4},{0,6},{14,8},{12,10},{10,12},{8,14},{7,1},{5,3},... | collective-permute-start | bytes 12296 | tf_op jit(solution)/shard_map/ppermute | solution.py:346
  66.4 4.3 %collective-permute-start.28 = (f32[8,128]{1,0:T(8,128)S(1)}, f32[8,128]{1,0:T(8,128)S(1)}, u32[]{:S(2)}, u32[]{:S(2)}) collective-permute-start(f32[8,128]{1,0:T(8,128)S(1)} %get-tuple-element.136.refs_0_), channel_id=1, source_target_pairs={{4,0},{6,2},{0,4},{2,6},{12,8},{14,10},{8,12},{10,14},{5,1},{7,3},... | collective-permute-start | bytes 12296 | tf_op jit(solution)/shard_map/ppermute | solution.py:346
  69.0 3.6 %collective-permute-start.27 = (f32[8,128]{1,0:T(8,128)S(1)}, f32[8,128]{1,0:T(8,128)S(1)}, u32[]{:S(2)}, u32[]{:S(2)}) collective-permute-start(f32[8,128]{1,0:T(8,128)S(1)} %get-tuple-element.136.refs_0_), channel_id=1, source_target_pairs={{2,0},{0,2},{6,4},{4,6},{10,8},{8,10},{14,12},{12,14},{3,1},{1,3},... | collective-permute-start | bytes 12296 | tf_op jit(solution)/shard_map/ppermute | solution.py:346
  73.0 1.8 %copy-start.28 = (bf16[32,2,2560]{2,1,0:T(2,128)(2,1)}, bf16[32,2,2560]{2,1,0:T(2,128)(2,1)S(1)}, u32[]{:S(2)}) copy-start(bf16[32,2,2560]{2,1,0:T(2,128)(2,1)S(1)} %get-tuple-element.97) | copy-start | bytes 983044
  73.1 1.2 %collective-permute-start.30 = (f32[1,224]{1,0:T(1,128)S(1)}, f32[1,224]{1,0:T(1,128)S(1)}, u32[]{:S(2)}, u32[]{:S(2)}) collective-permute-start(f32[1,224]{1,0:T(1,128)S(1)} %get-tuple-element.138), channel_id=1, source_target_pairs={{0,1},{1,0},{2,3},{3,2},{4,5},{5,4},{6,7},{7,6},{8,9},{9,8},{10,11... | collective-permute-start | bytes 2696 | tf_op jit(solution)/shard_map/ppermute | solution.py:379

commit v4 on v3

--- a/solution.py
+++ b/solution.py
@@ -15,7 +15,7 @@
 LANES = 128
 BLOCK = 256
 SHARES = (0.3, 0.4, 0.3)
-PIN = (0, 1, 2, 3)
+PIN = (1, 2, 3)
 KEEP = (0,)
 COST = 5
 FLOWS = (3, 1, 2)

time: 75 us -> 74.8 us (level)
    ppermute x3, waiting for transfers between devices: 3.22 us -> 2.45 us  [exchange(): lax.ppermute(gain, axes, [(b, a) for a, b in forward(part)])]
    unnamed x37 -> x35, local copies, waits for them, and re-layouts: 3.01 us -> 3 us
  transfers between devices with their start and end apart: 16 -> 16, of which waited for: 11 -> 9; matrix products, arithmetic and copies ran while one was open for 2% -> 2% of each run, Pallas kernels for 18% -> 18%
where the time goes in v4:
time: 74.8 us; the launch traced here: 74.6 us
  waiting for transfers between devices  26.2 us (35%)
  starting transfers between devices  25.2 us (34%)
  Pallas kernels  16.2 us (22%)
  local copies, waits for them, and re-layouts  3.75 us (5%)
  other arithmetic  1.59 us (2%)
  between operations  1.52 us (2%)
    pallas_call x10, Pallas kernels, call(): pl.pallas_call(kernel, in_specs=specs, out_specs=places, out_shape=shapes...  16.2 us
    ppermute x9, starting transfers between devices, deliver(): taken[part] = lax.ppermute(packed[part], axes, forward(part))  15.3 us
    ppermute x9, waiting for transfers between devices, deliver(): taken[part] = lax.ppermute(packed[part], axes, forward(part))  13.8 us
    ppermute x3, waiting for transfers between devices, exchange(): lax.ppermute(code, axes, across(step))  8.92 us
    ppermute x3, starting transfers between devices, exchange(): lax.ppermute(code, axes, across(step))  6.37 us
    ppermute x3, starting transfers between devices, exchange(): lax.ppermute(gain, axes, [(b, a) for a, b in forward(part)])  3.5 us
    unnamed x35, local copies, waits for them, and re-layouts  3 us
    ppermute x3, waiting for transfers between devices, exchange(): lax.ppermute(gain, axes, [(b, a) for a, b in forward(part)])  2.45 us
  transfers between devices with their start and end apart: 16, of which 9 were waited for; matrix products, arithmetic and copies ran while one was open for 2% of the time, Pallas kernels for 18%

profile of v4, /device:TPU:0, one launch (start us, length us, event | category | flops | bytes accessed | tf_op | source)
XLA Modules:
  0.0 74.6 jit_solution(10116852989368573205)
XLA Ops:
  0.7 2.0 %copy.7 = bf16[28,8,2,2560]{3,1,2,0:T(8,128)(2,1)S(1)} copy(bf16[28,8,2,2560]{3,2,1,0:T(2,128)(2,1)} %bitcast.23) | data formatting | bytes 4587520
  2.7 1.4 %shard_map.59 = (bf16[72,1664]{1,0:T(8,128)(2,1)}, bf16[72,1664]{1,0:T(8,128)(2,1)}, bf16[72,1664]{1,0:T(8,128)(2,1)}, bf16[72,1664]{1,0:T(8,128)(2,1)}, s32[8,224]{1,0:T(8,128)S(1)}) custom-call(bf16[224,5120]{1,0:T(8,128)(2,1)S(1)} %bitcast.17, s32[1,224]{1,0:T(1,128)S(1)} %bitcast.26, s32[1,224]{1,0:T(1,128)S(1)} %bitcast.28, s32[1,224]{1,0:T(1,128)S(1)} %bitcast.30, ...), custom_call_target="tpu_custom_call" | custom-call | flops 15000000512 | tf_op jit(solution)/shard_map/pallas_call | solution.py:235
  4.1 2.9 %collective-permute-start.15 = (bf16[72,1664]{1,0:T(8,128)(2,1)}, bf16[72,1664]{1,0:T(8,128)(2,1)}, u32[]{:S(2)}, u32[]{:S(2)}) collective-permute-start(bf16[72,1664]{1,0:T(8,128)(2,1)} %get-tuple-element.101), channel_id=1, source_target_pairs={{0,2},{2,0},{4,6},{6,4},{8,10},{10,8},{12,14},{14,12},{1,3},{3,1},... | collective-permute-start | bytes 718856 | tf_op jit(solution)/shard_map/ppermute | solution.py:269
  7.1 1.6 %collective-permute-start.16 = (bf16[72,1664]{1,0:T(8,128)(2,1)}, bf16[72,1664]{1,0:T(8,128)(2,1)}, u32[]{:S(2)}, u32[]{:S(2)}) collective-permute-start(bf16[72,1664]{1,0:T(8,128)(2,1)} %get-tuple-element.102), channel_id=1, source_target_pairs={{0,4},{2,6},{4,0},{6,2},{8,12},{10,14},{12,8},{14,10},{1,5},{3,7},... | collective-permute-start | bytes 718856 | tf_op jit(solution)/shard_map/ppermute | solution.py:269
  8.6 0.0 collective-permute-start.17
  8.7 1.2 %shard_map.62 = (bf16[72,2048]{1,0:T(8,128)(2,1)}, bf16[72,2048]{1,0:T(8,128)(2,1)}, bf16[72,2048]{1,0:T(8,128)(2,1)S(1)}, bf16[72,2048]{1,0:T(8,128)(2,1)S(1)}) custom-call(s32[8,224]{1,0:T(8,128)S(1)} %get-tuple-element.125.slot_ref, bf16[224,5120]{1,0:T(8,128)(2,1)S(1)} %bitcast.18), custom_call_target="tpu_custom_call" | custom-call | flops 5000000000 | tf_op jit(solution)/shard_map/pallas_call | solution.py:235
  9.9 1.9 %collective-permute-start.19 = (bf16[72,2048]{1,0:T(8,128)(2,1)}, bf16[72,2048]{1,0:T(8,128)(2,1)S(1)}, u32[]{:S(2)}, u32[]{:S(2)}) collective-permute-start(bf16[72,2048]{1,0:T(8,128)(2,1)} %get-tuple-element.114), channel_id=1, source_target_pairs={{0,2},{2,0},{4,6},{6,4},{8,10},{10,8},{12,14},{14,12},{1,3},{3,1},... | collective-permute-start | bytes 884744 | tf_op jit(solution)/shard_map/ppermute | solution.py:269
  11.8 1.6 %collective-permute-start.20 = (bf16[72,2048]{1,0:T(8,128)(2,1)S(1)}, bf16[72,2048]{1,0:T(8,128)(2,1)S(1)}, u32[]{:S(2)}, u32[]{:S(2)}) collective-permute-start(bf16[72,2048]{1,0:T(8,128)(2,1)S(1)} %get-tuple-element.115), channel_id=1, source_target_pairs={{0,4},{2,6},{4,0},{6,2},{8,12},{10,14},{12,8},{14,10},{1,5},{3,7},... | collective-permute-start | bytes 884744 | tf_op jit(solution)/shard_map/ppermute | solution.py:269
  13.3 1.4 %collective-permute-done.15.refs_1_ = bf16[72,1664]{1,0:T(8,128)(2,1)} collective-permute-done((bf16[72,1664]{1,0:T(8,128)(2,1)}, bf16[72,1664]{1,0:T(8,128)(2,1)}, u32[]{:S(2)}, u32[]{:S(2)}) %collective-permute-start.15) | collective-permute-done | bytes 239648 | tf_op jit(solution)/shard_map/ppermute | solution.py:269
  14.7 3.8 %collective-permute-start.21 = (bf16[72,2048]{1,0:T(8,128)(2,1)S(1)}, bf16[72,2048]{1,0:T(8,128)(2,1)S(1)}, u32[]{:S(2)}, u32[]{:S(2)}) collective-permute-start(bf16[72,2048]{1,0:T(8,128)(2,1)S(1)} %get-tuple-element.116), channel_id=1, source_target_pairs={{0,6},{2,4},{4,2},{6,0},{8,14},{10,12},{12,10},{14,8},{1,7},{3,5},... | collective-permute-start | bytes 884744 | tf_op jit(solution)/shard_map/ppermute | solution.py:269
  18.5 0.0 collective-permute-done.16.refs_2_
  18.5 2.3 %collective-permute-done.17.refs_3_ = bf16[72,1664]{1,0:T(8,128)(2,1)} collective-permute-done((bf16[72,1664]{1,0:T(8,128)(2,1)}, bf16[72,1664]{1,0:T(8,128)(2,1)}, u32[]{:S(2)}, u32[]{:S(2)}) %collective-permute-start.17) | collective-permute-done | bytes 239648 | tf_op jit(solution)/shard_map/ppermute | solution.py:269
  20.8 0.9 %copy-done.27 = bf16[72,1664]{1,0:T(8,128)(2,1)S(1)} copy-done((bf16[72,1664]{1,0:T(8,128)(2,1)S(1)}, bf16[72,1664]{1,0:T(8,128)(2,1)}, u32[]{:S(2)}) %copy-start.27) | copy-done | bytes 239640
  21.8 4.3 %shard_map.60 = (s16[64,1664]{1,0:T(8,128)(2,1)S(1)}, f32[64,1536]{1,0:T(8,128)}, bf16[288,1536]{1,0:T(8,128)(2,1)}, bf16[288,1536]{1,0:T(8,128)(2,1)}, bf16[288...) custom-call(bf16[72,1664]{1,0:T(8,128)(2,1)S(1)} %copy-done.27, ...), custom_call_target="tpu_custom_call" | custom-call | flops 20000000000 | tf_op jit(solution)/shard_map/pallas_call | solution.py:235
  26.0 3.1 %collective-permute-start.18 = (s16[64,1664]{1,0:T(8,128)(2,1)S(1)}, s16[64,1664]{1,0:T(8,128)(2,1)S(1)}, u32[]{:S(2)}, u32[]{:S(2)}) collective-permute-start(s16[64,1664]{1,0:T(8,128)(2,1)S(1)} %get-tuple-element.105), channel_id=1, source_target_pairs={{0,8},{2,10},{4,12},{6,14},{8,0},{10,2},{12,4},{14,6},{1,9},{3,11}... | collective-permute-start | bytes 638984 | tf_op jit(solution)/shard_map/ppermute | solution.py:324
  29.1 1.0 %shard_map.65 = (bf16[72,1536]{1,0:T(8,128)(2,1)}, bf16[72,1536]{1,0:T(8,128)(2,1)S(1)}, bf16[72,1536]{1,0:T(8,128)(2,1)S(1)}, bf16[72,1536]{1,0:T(8,128)(2,1)S(1)}) custom-call(s32[8,224]{1,0:T(8,128)S(1)} %get-tuple-element.125.slot_ref, bf16[224,5120]{1,0:T(8,128)(2,1)S(1)} %bitcast.19), custom_call_target="tpu_custom_call" | custom-call | flops 5000000000 | tf_op jit(solution)/shard_map/pallas_call | solution.py:235
  30.1 1.5 %collective-permute-start.23 = (bf16[72,1536]{1,0:T(8,128)(2,1)S(1)}, bf16[72,1536]{1,0:T(8,128)(2,1)S(1)}, u32[]{:S(2)}, u32[]{:S(2)}) collective-permute-start(bf16[72,1536]{1,0:T(8,128)(2,1)S(1)} %get-tuple-element.127), channel_id=1, source_target_pairs={{0,2},{2,0},{4,6},{6,4},{8,10},{10,8},{12,14},{14,12},{1,3},{3,1},... | collective-permute-start | bytes 663560 | tf_op jit(solution)/shard_map/ppermute | solution.py:269
  31.6 0.0 collective-permute-done.19.refs_1_
  31.6 1.6 %collective-permute-start.24 = (bf16[72,1536]{1,0:T(8,128)(2,1)S(1)}, bf16[72,1536]{1,0:T(8,128)(2,1)S(1)}, u32[]{:S(2)}, u32[]{:S(2)}) collective-permute-start(bf16[72,1536]{1,0:T(8,128)(2,1)S(1)} %get-tuple-element.128), channel_id=1, source_target_pairs={{0,4},{2,6},{4,0},{6,2},{8,12},{10,14},{12,8},{14,10},{1,5},{3,7},... | collective-permute-start | bytes 663560 | tf_op jit(solution)/shard_map/ppermute | solution.py:269
  33.1 0.0 collective-permute-done.20.refs_2_
  33.1 0.4 collective-permute-start.25
  33.6 4.4 %collective-permute-done.21.refs_3_ = bf16[72,2048]{1,0:T(8,128)(2,1)S(1)} collective-permute-done((bf16[72,2048]{1,0:T(8,128)(2,1)S(1)}, bf16[72,2048]{1,0:T(8,128)(2,1)S(1)}, u32[]{:S(2)}, u32[]{:S(2)}) %collective-permute-start.21) | collective-permute-done | bytes 294944 | tf_op jit(solution)/shard_map/ppermute | solution.py:269
  38.0 3.1 %shard_map.63 = (s16[64,2176]{1,0:T(8,128)(2,1)S(1)}, f32[64,2048]{1,0:T(8,128)}, bf16[288,2048]{1,0:T(8,128)(2,1)}, bf16[288,2048]{1,0:T(8,128)(2,1)}) custom-call(bf16[72,2048]{1,0:T(8,128)(2,1)S(1)} %copy-done.21, bf16[72,2048]{1,0:T(8,128)(2,1)S(1)} %collective-permute-done.19.refs_1_, bf16[72,2048]{1,0:T(8,128)(2,1)S(1)} %collective-permute-done.20.refs_2_, ...), custom_call_target="tpu_custom_call" | custom-call | flops 15000000512 | tf_op jit(solution)/shard_map/pallas_call | solution.py:235
  41.1 2.1 %collective-permute-start.22 = (s16[64,2176]{1,0:T(8,128)(2,1)S(1)}, s16[64,2176]{1,0:T(8,128)(2,1)S(1)}, u32[]{:S(2)}, u32[]{:S(2)}) collective-permute-start(s16[64,2176]{1,0:T(8,128)(2,1)S(1)} %get-tuple-element.119), channel_id=1, source_target_pairs={{0,8},{2,10},{4,12},{6,14},{8,0},{10,2},{12,4},{14,6},{1,9},{3,11}... | collective-permute-start | bytes 835592 | tf_op jit(solution)/shard_map/ppermute | solution.py:324
  43.2 0.0 collective-permute-done.18.refs_0_
  43.2 0.7 shard_map.61
  44.0 0.6 slice.3
  45.2 0.0 collective-permute-done.23.refs_1_
  45.2 3.1 %collective-permute-done.24.refs_2_ = bf16[72,1536]{1,0:T(8,128)(2,1)S(1)} collective-permute-done((bf16[72,1536]{1,0:T(8,128)(2,1)S(1)}, bf16[72,1536]{1,0:T(8,128)(2,1)S(1)}, u32[]{:S(2)}, u32[]{:S(2)}) %collective-permute-start.24) | collective-permute-done | bytes 221216 | tf_op jit(solution)/shard_map/ppermute | solution.py:269
  48.3 2.6 %collective-permute-done.25.refs_3_ = bf16[72,1536]{1,0:T(8,128)(2,1)S(1)} collective-permute-done((bf16[72,1536]{1,0:T(8,128)(2,1)S(1)}, bf16[72,1536]{1,0:T(8,128)(2,1)S(1)}, u32[]{:S(2)}, u32[]{:S(2)}) %collective-permute-start.25) | collective-permute-done | bytes 221216 | tf_op jit(solution)/shard_map/ppermute | solution.py:269
  50.9 2.4 %shard_map.66 = (s16[64,1664]{1,0:T(8,128)(2,1)S(1)}, f32[64,1536]{1,0:T(8,128)}, bf16[288,1536]{1,0:T(8,128)(2,1)}, bf16[288,1536]{1,0:T(8,128)(2,1)}) custom-call(bf16[72,1536]{1,0:T(8,128)(2,1)S(1)} %copy-done.22, bf16[72,1536]{1,0:T(8,128)(2,1)S(1)} %collective-permute-done.23.refs_1_, bf16[72,1536]{1,0:T(8,128)(2,1)S(1)} %collective-permute-done.24.refs_2_, ...), custom_call_target="tpu_custom_call" | custom-call | flops 15000000512 | tf_op jit(solution)/shard_map/pallas_call | solution.py:235
  53.4 1.2 %collective-permute-start.26 = (s16[64,1664]{1,0:T(8,128)(2,1)S(1)}, s16[64,1664]{1,0:T(8,128)(2,1)S(1)}, u32[]{:S(2)}, u32[]{:S(2)}) collective-permute-start(s16[64,1664]{1,0:T(8,128)(2,1)S(1)} %get-tuple-element.130), channel_id=1, source_target_pairs={{0,8},{2,10},{4,12},{6,14},{8,0},{10,2},{12,4},{14,6},{1,9},{3,11}... | collective-permute-start | bytes 638984 | tf_op jit(solution)/shard_map/ppermute | solution.py:324
  54.6 0.9 %shard_map.64 = (bf16[64,2048]{1,0:T(8,128)(2,1)S(1)}, f32[8,288]{1,0:T(8,128)S(1)}) custom-call(s16[64,2176]{1,0:T(8,128)(2,1)S(1)} %collective-permute-done.22.refs_0_, f32[64,2048]{1,0:T(8,128)S(1)} %copy-done.14, bf16[288,2048]{1,0:T(8,128)(2,1)S(1)} %copy-done.7, bf16[288,2048]{1,0:T(8,128)(2,1)S(1)} %copy-done.8, bf16[2,64,288]{2,1,0:T(8,128)(2,1)S(1)} %copy-done.24, ...), custom_call_target="tpu_custom_call" | custom-call | flops 5000000000 | tf_op jit(solution)/shard_map/pallas_call | solution.py:235
  55.5 0.1 reshape.62
  55.6 8.9 %collective-permute-done.26.refs_0_ = s16[64,1664]{1,0:T(8,128)(2,1)S(1)} collective-permute-done((s16[64,1664]{1,0:T(8,128)(2,1)S(1)}, s16[64,1664]{1,0:T(8,128)(2,1)S(1)}, u32[]{:S(2)}, u32[]{:S(2)}) %collective-permute-start.26) | collective-permute-done | bytes 213024 | tf_op jit(solution)/shard_map/ppermute | solution.py:324
  64.6 0.8 %shard_map.67 = (bf16[64,1536]{1,0:T(8,128)(2,1)S(1)}, f32[8,128]{1,0:T(8,128)S(1)}) custom-call(s16[64,1664]{1,0:T(8,128)(2,1)S(1)} %collective-permute-done.26.refs_0_, f32[64,1536]{1,0:T(8,128)S(1)} %copy-done.18, bf16[288,1536]{1,0:T(8,128)(2,1)S(1)} %copy-done.9, bf16[288,1536]{1,0:T(8,128)(2,1)S(1)} %copy-done.10, bf16[2,64,288]{2,1,0:T(8,128)(2,1)S(1)} %copy-done.25, ...), custom_call_target="tpu_custom_call" | custom-call | flops 5000000000 | tf_op jit(solution)/shard_map/pallas_call | solution.py:235
  65.4 0.9 %collective-permute-start.29 = (f32[8,128]{1,0:T(8,128)S(1)}, f32[8,128]{1,0:T(8,128)S(1)}, u32[]{:S(2)}, u32[]{:S(2)}) collective-permute-start(f32[8,128]{1,0:T(8,128)S(1)} %get-tuple-element.136.refs_0_), channel_id=1, source_target_pairs={{6,0},{4,2},{2,4},{0,6},{14,8},{12,10},{10,12},{8,14},{7,1},{5,3},... | collective-permute-start | bytes 12296 | tf_op jit(solution)/shard_map/ppermute | solution.py:346
  66.3 2.6 %collective-permute-start.28 = (f32[8,128]{1,0:T(8,128)S(1)}, f32[8,128]{1,0:T(8,128)S(1)}, u32[]{:S(2)}, u32[]{:S(2)}) collective-permute-start(f32[8,128]{1,0:T(8,128)S(1)} %get-tuple-element.136.refs_0_), channel_id=1, source_target_pairs={{4,0},{6,2},{0,4},{2,6},{12,8},{14,10},{8,12},{10,14},{5,1},{7,3},... | collective-permute-start | bytes 12296 | tf_op jit(solution)/shard_map/ppermute | solution.py:346
  68.8 0.1 collective-permute-start.27
  69.0 1.0 %pad_maximum_fusion.1 = bf16[32,2,2560]{2,1,0:T(2,128)(2,1)} fusion(bf16[32,2,768]{2,1,0:T(2,128)(2,1)S(1)} %reshape.63, bf16[32,2,1024]{2,1,0:T(2,128)(2,1)S(1)} %reshape.62, bf16[32,2,768]{2,1,0:T(2,128)(2,1)S(1)} %reshape.61), kind=kLoop, calls=%fused_computation.4 | loop fusion | flops 983040 | bytes 655360 | tf_op jit(solution)/shard_map/concatenate | solution.py:351
  70.0 0.0 collective-permute-done.29.refs_3_
  70.0 0.5 collective-permute-done.28.refs_2_
  70.5 2.0 %collective-permute-done.27.refs_1_ = f32[8,128]{1,0:T(8,128)S(1)} collective-permute-done((f32[8,128]{1,0:T(8,128)S(1)}, f32[8,128]{1,0:T(8,128)S(1)}, u32[]{:S(2)}, u32[]{:S(2)}) %collective-permute-start.27) | collective-permute-done | bytes 4128 | tf_op jit(solution)/shard_map/ppermute | solution.py:346
  72.5 0.3 shard_map.68
  72.7 0.1 conditional.1
  72.8 0.1 collective-permute-start.30
  72.9 1.1 %collective-permute-done.30 = f32[1,224]{1,0:T(1,128)S(1)} collective-permute-done((f32[1,224]{1,0:T(1,128)S(1)}, f32[1,224]{1,0:T(1,128)S(1)}, u32[]{:S(2)}, u32[]{:S(2)}) %collective-permute-start.30) | collective-permute-done | bytes 928 | tf_op jit(solution)/shard_map/ppermute | solution.py:379
  74.0 0.6 add.16
  (38 shorter events, 0.2 us)
Async XLA Ops:
  0.6 2.0 %copy-start.28 = (s32[224,1]{0,1:T(1,128)S(1)}, s32[224,1]{0,1:T(1,128)}, u32[]{:S(2)}) copy-start(s32[224,1]{0,1:T(1,128)} %param.7) | copy-start | bytes 2692
  0.6 2.0 %copy-start.29 = (s32[224]{0:T(256)S(1)}, s32[224]{0:T(256)}, u32[]{:S(2)}) copy-start(s32[224]{0:T(256)} %param.8) | copy-start | bytes 2692
  0.7 2.0 %copy-start.30 = (s32[224]{0:T(256)S(1)}, s32[224]{0:T(256)}, u32[]{:S(2)}) copy-start(s32[224]{0:T(256)} %param.9) | copy-start | bytes 2692
  4.1 10.6 %collective-permute-start.15 = (bf16[72,1664]{1,0:T(8,128)(2,1)}, bf16[72,1664]{1,0:T(8,128)(2,1)}, u32[]{:S(2)}, u32[]{:S(2)}) collective-permute-start(bf16[72,1664]{1,0:T(8,128)(2,1)} %get-tuple-element.101), channel_id=1, source_target_pairs={{0,2},{2,0},{4,6},{6,4},{8,10},{10,8},{12,14},{14,12},{1,3},{3,1},... | collective-permute-start | bytes 718856 | tf_op jit(solution)/shard_map/ppermute | solution.py:269
  7.1 11.5 %collective-permute-start.16 = (bf16[72,1664]{1,0:T(8,128)(2,1)}, bf16[72,1664]{1,0:T(8,128)(2,1)}, u32[]{:S(2)}, u32[]{:S(2)}) collective-permute-start(bf16[72,1664]{1,0:T(8,128)(2,1)} %get-tuple-element.102), channel_id=1, source_target_pairs={{0,4},{2,6},{4,0},{6,2},{8,12},{10,14},{12,8},{14,10},{1,5},{3,7},... | collective-permute-start | bytes 718856 | tf_op jit(solution)/shard_map/ppermute | solution.py:269
  8.6 12.2 %collective-permute-start.17 = (bf16[72,1664]{1,0:T(8,128)(2,1)}, bf16[72,1664]{1,0:T(8,128)(2,1)}, u32[]{:S(2)}, u32[]{:S(2)}) collective-permute-start(bf16[72,1664]{1,0:T(8,128)(2,1)} %get-tuple-element.103), channel_id=1, source_target_pairs={{0,6},{2,4},{4,2},{6,0},{8,14},{10,12},{12,10},{14,8},{1,7},{3,5},... | collective-permute-start | bytes 718856 | tf_op jit(solution)/shard_map/ppermute | solution.py:269
  9.9 21.7 %collective-permute-start.19 = (bf16[72,2048]{1,0:T(8,128)(2,1)}, bf16[72,2048]{1,0:T(8,128)(2,1)S(1)}, u32[]{:S(2)}, u32[]{:S(2)}) collective-permute-start(bf16[72,2048]{1,0:T(8,128)(2,1)} %get-tuple-element.114), channel_id=1, source_target_pairs={{0,2},{2,0},{4,6},{6,4},{8,10},{10,8},{12,14},{14,12},{1,3},{3,1},... | collective-permute-start | bytes 884744 | tf_op jit(solution)/shard_map/ppermute | solution.py:269
  11.8 21.4 %collective-permute-start.20 = (bf16[72,2048]{1,0:T(8,128)(2,1)S(1)}, bf16[72,2048]{1,0:T(8,128)(2,1)S(1)}, u32[]{:S(2)}, u32[]{:S(2)}) collective-permute-start(bf16[72,2048]{1,0:T(8,128)(2,1)S(1)} %get-tuple-element.115), channel_id=1, source_target_pairs={{0,4},{2,6},{4,0},{6,2},{8,12},{10,14},{12,8},{14,10},{1,5},{3,7},... | collective-permute-start | bytes 884744 | tf_op jit(solution)/shard_map/ppermute | solution.py:269
  14.7 23.2 %collective-permute-start.21 = (bf16[72,2048]{1,0:T(8,128)(2,1)S(1)}, bf16[72,2048]{1,0:T(8,128)(2,1)S(1)}, u32[]{:S(2)}, u32[]{:S(2)}) collective-permute-start(bf16[72,2048]{1,0:T(8,128)(2,1)S(1)} %get-tuple-element.116), channel_id=1, source_target_pairs={{0,6},{2,4},{4,2},{6,0},{8,14},{10,12},{12,10},{14,8},{1,7},{3,5},... | collective-permute-start | bytes 884744 | tf_op jit(solution)/shard_map/ppermute | solution.py:269
  20.8 0.9 %copy-start.27 = (bf16[72,1664]{1,0:T(8,128)(2,1)S(1)}, bf16[72,1664]{1,0:T(8,128)(2,1)}, u32[]{:S(2)}) copy-start(bf16[72,1664]{1,0:T(8,128)(2,1)} %get-tuple-element.100.refs_0_) | copy-start | bytes 718852
  26.0 11.9 %copy-start.21 = (bf16[72,2048]{1,0:T(8,128)(2,1)S(1)}, bf16[72,2048]{1,0:T(8,128)(2,1)}, u32[]{:S(2)}) copy-start(bf16[72,2048]{1,0:T(8,128)(2,1)} %get-tuple-element.113.refs_0_) | copy-start | bytes 884740
  26.0 11.9 %copy-start.24 = (bf16[2,64,288]{2,1,0:T(8,128)(2,1)S(1)}, bf16[2,64,288]{2,1,0:T(8,128)(2,1)}, u32[]{:S(2)}) copy-start(bf16[2,64,288]{2,1,0:T(8,128)(2,1)} %get-tuple-element.109.refs_4_.refs_6_) | copy-start | bytes 221188
  26.0 17.2 %collective-permute-start.18 = (s16[64,1664]{1,0:T(8,128)(2,1)S(1)}, s16[64,1664]{1,0:T(8,128)(2,1)S(1)}, u32[]{:S(2)}, u32[]{:S(2)}) collective-permute-start(s16[64,1664]{1,0:T(8,128)(2,1)S(1)} %get-tuple-element.105), channel_id=1, source_target_pairs={{0,8},{2,10},{4,12},{6,14},{8,0},{10,2},{12,4},{14,6},{1,9},{3,11}... | collective-permute-start | bytes 638984 | tf_op jit(solution)/shard_map/ppermute | solution.py:324
  30.1 15.2 %collective-permute-start.23 = (bf16[72,1536]{1,0:T(8,128)(2,1)S(1)}, bf16[72,1536]{1,0:T(8,128)(2,1)S(1)}, u32[]{:S(2)}, u32[]{:S(2)}) collective-permute-start(bf16[72,1536]{1,0:T(8,128)(2,1)S(1)} %get-tuple-element.127), channel_id=1, source_target_pairs={{0,2},{2,0},{4,6},{6,4},{8,10},{10,8},{12,14},{14,12},{1,3},{3,1},... | collective-permute-start | bytes 663560 | tf_op jit(solution)/shard_map/ppermute | solution.py:269
  31.6 16.8 %collective-permute-start.24 = (bf16[72,1536]{1,0:T(8,128)(2,1)S(1)}, bf16[72,1536]{1,0:T(8,128)(2,1)S(1)}, u32[]{:S(2)}, u32[]{:S(2)}) collective-permute-start(bf16[72,1536]{1,0:T(8,128)(2,1)S(1)} %get-tuple-element.128), channel_id=1, source_target_pairs={{0,4},{2,6},{4,0},{6,2},{8,12},{10,14},{12,8},{14,10},{1,5},{3,7},... | collective-permute-start | bytes 663560 | tf_op jit(solution)/shard_map/ppermute | solution.py:269
  33.1 17.8 %collective-permute-start.25 = (bf16[72,1536]{1,0:T(8,128)(2,1)S(1)}, bf16[72,1536]{1,0:T(8,128)(2,1)S(1)}, u32[]{:S(2)}, u32[]{:S(2)}) collective-permute-start(bf16[72,1536]{1,0:T(8,128)(2,1)S(1)} %get-tuple-element.129), channel_id=1, source_target_pairs={{0,6},{2,4},{4,2},{6,0},{8,14},{10,12},{12,10},{14,8},{1,7},{3,5},... | collective-permute-start | bytes 663560 | tf_op jit(solution)/shard_map/ppermute | solution.py:269
  38.0 5.3 %copy-start.11 = (bf16[288,1536]{1,0:T(8,128)(2,1)S(1)}, bf16[288,1536]{1,0:T(8,128)(2,1)}, u32[]{:S(2)}) copy-start(bf16[288,1536]{1,0:T(8,128)(2,1)} %get-tuple-element.107.refs_2_) | copy-start | bytes 2654212
  38.0 5.3 %copy-start.12 = (bf16[288,1536]{1,0:T(8,128)(2,1)S(1)}, bf16[288,1536]{1,0:T(8,128)(2,1)}, u32[]{:S(2)}) copy-start(bf16[288,1536]{1,0:T(8,128)(2,1)} %get-tuple-element.108.refs_3_) | copy-start | bytes 2654212
  38.0 5.3 %copy-start.19 = (f32[64,1536]{1,0:T(8,128)S(1)}, f32[64,1536]{1,0:T(8,128)}, u32[]{:S(2)}) copy-start(f32[64,1536]{1,0:T(8,128)} %get-tuple-element.106.refs_1_) | copy-start | bytes 1179652
  41.1 13.4 %collective-permute-start.22 = (s16[64,2176]{1,0:T(8,128)(2,1)S(1)}, s16[64,2176]{1,0:T(8,128)(2,1)S(1)}, u32[]{:S(2)}, u32[]{:S(2)}) collective-permute-start(s16[64,2176]{1,0:T(8,128)(2,1)S(1)} %get-tuple-element.119), channel_id=1, source_target_pairs={{0,8},{2,10},{4,12},{6,14},{8,0},{10,2},{12,4},{14,6},{1,9},{3,11}... | collective-permute-start | bytes 835592 | tf_op jit(solution)/shard_map/ppermute | solution.py:324
  43.2 7.7 %copy-start.22 = (bf16[72,1536]{1,0:T(8,128)(2,1)S(1)}, bf16[72,1536]{1,0:T(8,128)(2,1)}, u32[]{:S(2)}) copy-start(bf16[72,1536]{1,0:T(8,128)(2,1)} %get-tuple-element.126.refs_0_) | copy-start | bytes 663556
  50.9 3.6 %copy-start.7 = (bf16[288,2048]{1,0:T(8,128)(2,1)S(1)}, bf16[288,2048]{1,0:T(8,128)(2,1)}, u32[]{:S(2)}) copy-start(bf16[288,2048]{1,0:T(8,128)(2,1)} %get-tuple-element.121.refs_2_) | copy-start | bytes 3538948
  50.9 3.6 %copy-start.8 = (bf16[288,2048]{1,0:T(8,128)(2,1)S(1)}, bf16[288,2048]{1,0:T(8,128)(2,1)}, u32[]{:S(2)}) copy-start(bf16[288,2048]{1,0:T(8,128)(2,1)} %get-tuple-element.122.refs_3_) | copy-start | bytes 3538948
  50.9 3.6 %copy-start.14 = (f32[64,2048]{1,0:T(8,128)S(1)}, f32[64,2048]{1,0:T(8,128)}, u32[]{:S(2)}) copy-start(f32[64,2048]{1,0:T(8,128)} %get-tuple-element.120.refs_1_) | copy-start | bytes 1572868
  53.4 11.2 %collective-permute-start.26 = (s16[64,1664]{1,0:T(8,128)(2,1)S(1)}, s16[64,1664]{1,0:T(8,128)(2,1)S(1)}, u32[]{:S(2)}, u32[]{:S(2)}) collective-permute-start(s16[64,1664]{1,0:T(8,128)(2,1)S(1)} %get-tuple-element.130), channel_id=1, source_target_pairs={{0,8},{2,10},{4,12},{6,14},{8,0},{10,2},{12,4},{14,6},{1,9},{3,11}... | collective-permute-start | bytes 638984 | tf_op jit(solution)/shard_map/ppermute | solution.py:324
  54.5 10.0 %copy-start.9 = (bf16[288,1536]{1,0:T(8,128)(2,1)S(1)}, bf16[288,1536]{1,0:T(8,128)(2,1)}, u32[]{:S(2)}) copy-start(bf16[288,1536]{1,0:T(8,128)(2,1)} %get-tuple-element.132.refs_2_) | copy-start | bytes 2654212
  54.5 10.0 %copy-start.10 = (bf16[288,1536]{1,0:T(8,128)(2,1)S(1)}, bf16[288,1536]{1,0:T(8,128)(2,1)}, u32[]{:S(2)}) copy-start(bf16[288,1536]{1,0:T(8,128)(2,1)} %get-tuple-element.133.refs_3_) | copy-start | bytes 2654212
  54.6 10.0 %copy-start.18 = (f32[64,1536]{1,0:T(8,128)S(1)}, f32[64,1536]{1,0:T(8,128)}, u32[]{:S(2)}) copy-start(f32[64,1536]{1,0:T(8,128)} %get-tuple-element.131.refs_1_) | copy-start | bytes 1179652
  54.6 10.0 %copy-start.25 = (bf16[2,64,288]{2,1,0:T(8,128)(2,1)S(1)}, bf16[2,64,288]{2,1,0:T(8,128)(2,1)}, u32[]{:S(2)}) copy-start(bf16[2,64,288]{2,1,0:T(8,128)(2,1)} %get-tuple-element.109.refs_4_.refs_6_) | copy-start | bytes 221188
  65.4 4.6 %collective-permute-start.29 = (f32[8,128]{1,0:T(8,128)S(1)}, f32[8,128]{1,0:T(8,128)S(1)}, u32[]{:S(2)}, u32[]{:S(2)}) collective-permute-start(f32[8,128]{1,0:T(8,128)S(1)} %get-tuple-element.136.refs_0_), channel_id=1, source_target_pairs={{6,0},{4,2},{2,4},{0,6},{14,8},{12,10},{10,12},{8,14},{7,1},{5,3},... | collective-permute-start | bytes 12296 | tf_op jit(solution)/shard_map/ppermute | solution.py:346
  66.3 4.2 %collective-permute-start.28 = (f32[8,128]{1,0:T(8,128)S(1)}, f32[8,128]{1,0:T(8,128)S(1)}, u32[]{:S(2)}, u32[]{:S(2)}) collective-permute-start(f32[8,128]{1,0:T(8,128)S(1)} %get-tuple-element.136.refs_0_), channel_id=1, source_target_pairs={{4,0},{6,2},{0,4},{2,6},{12,8},{14,10},{8,12},{10,14},{5,1},{7,3},... | collective-permute-start | bytes 12296 | tf_op jit(solution)/shard_map/ppermute | solution.py:346
  68.8 3.6 %collective-permute-start.27 = (f32[8,128]{1,0:T(8,128)S(1)}, f32[8,128]{1,0:T(8,128)S(1)}, u32[]{:S(2)}, u32[]{:S(2)}) collective-permute-start(f32[8,128]{1,0:T(8,128)S(1)} %get-tuple-element.136.refs_0_), channel_id=1, source_target_pairs={{2,0},{0,2},{6,4},{4,6},{10,8},{8,10},{14,12},{12,14},{3,1},{1,3},... | collective-permute-start | bytes 12296 | tf_op jit(solution)/shard_map/ppermute | solution.py:346
  72.8 1.2 %collective-permute-start.30 = (f32[1,224]{1,0:T(1,128)S(1)}, f32[1,224]{1,0:T(1,128)S(1)}, u32[]{:S(2)}, u32[]{:S(2)}) collective-permute-start(f32[1,224]{1,0:T(1,128)S(1)} %get-tuple-element.138), channel_id=1, source_target_pairs={{0,1},{1,0},{2,3},{3,2},{4,5},{5,4},{6,7},{7,6},{8,9},{9,8},{10,11... | collective-permute-start | bytes 2696 | tf_op jit(solution)/shard_map/ppermute | solution.py:379
